TPU v7x, 128 devices: a whole 4x4x4 slice. The times are simulated.
128 devices in a mesh: seq: 16 (over z, x), chan: 8 (over y, core).
Axes of the slice: x: 4, y: 4, z: 4, core: 2. Of those that a mesh axis runs over, the one named last changes fastest.
Arguments:
- hidden_in: bfloat16 [32768, 8192], P('seq', 'chan'), may hold values from -6 to 6
- projection: bfloat16 [3, 8192, 512], P(None, 'chan'), may hold values from -0.0625 to 0.0625
- filter_taps: bfloat16 [512, 32768], P('chan', 'seq'), may hold values from -1.1 to 1.1
Outputs:
- gated: bfloat16 [512, 32768], P('chan', 'seq')
All inputs are finite; a program needn't handle non-finite values.
Results may differ from a plain program's by a relative error of at most 0.007.
Values may be sent and summed in bfloat16 or wider, within the bound.
A program may use at most 128 MiB of HBM per device.

v0:
```python
import math

import jax
import jax.numpy as jnp
from jax import lax
from jax.sharding import PartitionSpec as P

TWO_PI = 2.0 * math.pi


def swapped(value, axis, apart):
    return lax.ppermute(value, axis, [(i, i ^ 1 << apart) for i in range(lax.axis_size(axis))])


def phase_of(numer, modulus):
    return TWO_PI / modulus * (numer % modulus).astype(jnp.float32)


def rotate(real_part, imag_part, phase, sign_value):
    cosine = jnp.cos(phase)
    sine = jnp.sin(phase)
    return (
        real_part * cosine + sign_value * imag_part * sine,
        imag_part * cosine - sign_value * real_part * sine,
    )


def dft_table(length):
    counter = jnp.arange(length, dtype=jnp.int32)
    return phase_of(counter[:, None] * counter[None, :], length)


def complex_product(form, real_part, imag_part, table, sign_value):
    cosine = jnp.cos(table)
    sine = jnp.sin(table)
    highest = lax.Precision.HIGHEST
    new_real = jnp.einsum(form, real_part, cosine, precision=highest) + sign_value * jnp.einsum(
        form, imag_part, sine, precision=highest
    )
    new_imag = jnp.einsum(form, imag_part, cosine, precision=highest) - sign_value * jnp.einsum(
        form, real_part, sine, precision=highest
    )
    return (new_real, new_imag)


def factor_pair(length):
    first_len = 1
    for candidate in range(1, math.isqrt(length) + 1):
        if length % candidate == 0:
            first_len = candidate
    return (first_len, length // first_len)


def inner_twiddle(first_len, second_len):
    rows_index = jnp.arange(first_len, dtype=jnp.int32)[:, None]
    cols_index = jnp.arange(second_len, dtype=jnp.int32)[None, :]
    return phase_of(rows_index * cols_index, first_len * second_len)


def inner_forward(real_part, imag_part):
    leading = real_part.shape[:-1]
    length = real_part.shape[-1]
    first_len, second_len = factor_pair(length)
    real_part = real_part.reshape(leading + (first_len, second_len))
    imag_part = imag_part.reshape(leading + (first_len, second_len))
    real_part, imag_part = complex_product(
        "...jb,jk->...kb", real_part, imag_part, dft_table(first_len), 1.0
    )
    real_part, imag_part = rotate(real_part, imag_part, inner_twiddle(first_len, second_len), 1.0)
    real_part, imag_part = complex_product(
        "...kb,bl->...kl", real_part, imag_part, dft_table(second_len), 1.0
    )
    return (real_part.reshape(leading + (length,)), imag_part.reshape(leading + (length,)))


def inner_inverse(real_part, imag_part):
    leading = real_part.shape[:-1]
    length = real_part.shape[-1]
    first_len, second_len = factor_pair(length)
    real_part = real_part.reshape(leading + (first_len, second_len))
    imag_part = imag_part.reshape(leading + (first_len, second_len))
    real_part, imag_part = complex_product(
        "...kl,bl->...kb", real_part, imag_part, dft_table(second_len), -1.0
    )
    real_part, imag_part = rotate(real_part, imag_part, inner_twiddle(first_len, second_len), -1.0)
    real_part, imag_part = complex_product(
        "...kb,jk->...jb", real_part, imag_part, dft_table(first_len), -1.0
    )
    return (real_part.reshape(leading + (length,)), imag_part.reshape(leading + (length,)))


def parity_of(ndim):
    return jnp.arange(2, dtype=jnp.int32).reshape((2,) + (1,) * (ndim - 1))


def forward_spectra(signals, outer_index, blocks, cross):
    length = signals.shape[-1]
    total_len = 2 * blocks * length
    real_part = signals[None]
    parity = parity_of(real_part.ndim)
    real_part, imag_part = rotate(
        real_part, jnp.zeros_like(real_part), phase_of(outer_index * parity, 2 * blocks), 1.0
    )
    real_part, imag_part, freq_index = cross(real_part, imag_part)
    inner_pos = jnp.arange(length, dtype=jnp.int32)
    real_part, imag_part = rotate(
        real_part, imag_part, phase_of(inner_pos * (2 * freq_index + parity), total_len), 1.0
    )
    real_part, imag_part = inner_forward(real_part, imag_part)
    return (real_part, imag_part, freq_index)


def signal_back(real_part, imag_part, freq_index, outer_index, blocks, cross_back):
    length = real_part.shape[-1]
    total_len = 2 * blocks * length
    parity = parity_of(real_part.ndim)
    real_part, imag_part = inner_inverse(real_part, imag_part)
    inner_pos = jnp.arange(length, dtype=jnp.int32)
    real_part, imag_part = rotate(
        real_part, imag_part, phase_of(inner_pos * (2 * freq_index + parity), total_len), -1.0
    )
    real_part, imag_part = cross_back(real_part, imag_part)
    real_part, imag_part = rotate(
        real_part, imag_part, phase_of(outer_index * parity, 2 * blocks), -1.0
    )
    return jnp.sum(real_part, axis=0) / total_len


def filtered(real_part, imag_part):
    signal_real, filter_real = (real_part[:, 0], real_part[:, 1])
    signal_imag, filter_imag = (imag_part[:, 0], imag_part[:, 1])
    return (
        signal_real * filter_real - signal_imag * filter_imag,
        signal_real * filter_imag + signal_imag * filter_real,
    )


def device_sections(real_part, imag_part):
    bit_count = lax.axis_size("seq").bit_length() - 1
    device = lax.axis_index("seq")
    for bit_index in reversed(range(bit_count)):
        half_span = 1 << bit_index
        upper_side = device >> bit_index & 1 == 1
        offset = device & half_span - 1
        other_real, other_imag = swapped((real_part, imag_part), "seq", bit_index)
        base_real = jnp.where(upper_side, other_real - real_part, real_part + other_real)
        base_imag = jnp.where(upper_side, other_imag - imag_part, imag_part + other_imag)
        phase = jnp.where(upper_side, phase_of(offset, 2 * half_span), 0.0)
        real_part, imag_part = rotate(base_real, base_imag, phase, 1.0)
    freq_index = jnp.zeros((), jnp.int32)
    for bit_index in range(bit_count):
        freq_index = freq_index | (device >> bit_index & 1) << bit_count - 1 - bit_index
    return (real_part, imag_part, freq_index)


def device_sections_back(real_part, imag_part):
    bit_count = lax.axis_size("seq").bit_length() - 1
    device = lax.axis_index("seq")
    for bit_index in range(bit_count):
        half_span = 1 << bit_index
        upper_side = device >> bit_index & 1 == 1
        offset = device & half_span - 1
        phase = jnp.where(upper_side, phase_of(offset, 2 * half_span), 0.0)
        sent_real, sent_imag = rotate(real_part, imag_part, phase, -1.0)
        other_real, other_imag = swapped((sent_real, sent_imag), "seq", bit_index)
        real_part = jnp.where(upper_side, other_real - sent_real, real_part + other_real)
        imag_part = jnp.where(upper_side, other_imag - sent_imag, imag_part + other_imag)
    return (real_part, imag_part)


def per_device(hidden_in, projection, filter_taps):
    projected = lax.psum_scatter(
        jnp.einsum("td,jdc->cjt", hidden_in, projection, preferred_element_type=jnp.float32),
        "chan",
        scatter_dimension=0,
        tiled=True,
    ).astype(jnp.bfloat16)
    gating = projected[:, 0]
    mixed = (projected[:, 1].astype(jnp.float32) * projected[:, 2].astype(jnp.float32)).astype(
        jnp.bfloat16
    )
    blocks = lax.axis_size("seq")
    signals = jnp.stack([mixed.astype(jnp.float32), filter_taps.astype(jnp.float32)])
    device = lax.axis_index("seq")
    real_part, imag_part, freq_index = forward_spectra(signals, device, blocks, device_sections)
    real_part, imag_part = filtered(real_part, imag_part)
    convolved = signal_back(real_part, imag_part, freq_index, device, blocks, device_sections_back)
    return (gating.astype(jnp.float32) * convolved).astype(jnp.bfloat16)


def solution(mesh):
    placed = (P("seq", "chan"), P(None, "chan", None), P("chan", "seq"))
    return jax.shard_map(
        per_device, mesh=mesh, in_specs=placed, out_specs=P("chan", "seq"), check_vma=False
    )
```

profile of v0, /device:TPU:8, one launch (start us, length us, event | category | flops | bytes accessed | tf_op | source)
XLA Modules:
  0.0 825.7 jit_solution(17597727179372433307)
XLA Ops:
  8.4 11.4 %convolution_bitcast_fusion = f32[512,3,2048]{2,0,1:T(8,128)} fusion(bf16[3,1024,512]{2,1,0:T(8,128)(2,1)S(1)} %copy-done, bf16[2048,1024]{1,0:T(8,128)(2,1)} %param.3), kind=kOutput, calls=%fused_computation | convolution fusion | flops 6442450944 | bytes 19922944 | tf_op jit(solution)/shard_map/td,jdc->cjt/dot_general | solution.py:173
  20.0 72.3 %reduce-scatter.2.cloned.1.call-done = f32[64,3,2048]{2,0,1:T(8,128)} async-done(((f32[512,3,2048]{2,0,1:T(8,128)}), f32[64,3,2048]{2,0,1:T(8,128)}) %reduce-scatter.2.cloned.1.call-update) | async-done | bytes 1572880 | tf_op jit(solution)/shard_map/reduce_scatter | solution.py:172
  100.4 46.3 %collective-permute-done = f32[2,2,64,2048]{3,2,1,0:T(8,128)} collective-permute-done((f32[2,2,64,2048]{3,2,1,0:T(8,128)}, f32[2,2,64,2048]{3,2,1,0:T(8,128)}, u32[]{:S(2)}, u32[]{:S(2)}) %collective-permute-start) | collective-permute-done | bytes 2097184 | tf_op jit(solution)/shard_map/ppermute | solution.py:12
  146.6 44.9 %collective-permute-done.1 = f32[2,2,64,2048]{3,2,1,0:T(8,128)} collective-permute-done((f32[2,2,64,2048]{3,2,1,0:T(8,128)S(1)}, f32[2,2,64,2048]{3,2,1,0:T(8,128)}, u32[]{:S(2)}, u32[]{:S(2)}) %collective-permute-start.1) | collective-permute-done | bytes 2097184 | tf_op jit(solution)/shard_map/ppermute | solution.py:12
  198.5 46.6 %collective-permute-done.2 = f32[2,2,64,2048]{3,2,1,0:T(8,128)} collective-permute-done((f32[2,2,64,2048]{3,2,1,0:T(8,128)}, f32[2,2,64,2048]{3,2,1,0:T(8,128)}, u32[]{:S(2)}, u32[]{:S(2)}) %collective-permute-start.2) | collective-permute-done | bytes 2097184 | tf_op jit(solution)/shard_map/ppermute | solution.py:12
  245.1 44.4 %collective-permute-done.3 = f32[2,2,64,2048]{3,2,1,0:T(8,128)} collective-permute-done((f32[2,2,64,2048]{3,2,1,0:T(8,128)S(1)}, f32[2,2,64,2048]{3,2,1,0:T(8,128)}, u32[]{:S(2)}, u32[]{:S(2)}) %collective-permute-start.3) | collective-permute-done | bytes 2097184 | tf_op jit(solution)/shard_map/ppermute | solution.py:12
  289.5 6.2 multiply_subtract_fusion.5
  299.4 46.7 %collective-permute-done.4 = f32[2,2,64,2048]{3,2,1,0:T(8,128)} collective-permute-done((f32[2,2,64,2048]{3,2,1,0:T(8,128)}, f32[2,2,64,2048]{3,2,1,0:T(8,128)}, u32[]{:S(2)}, u32[]{:S(2)}) %collective-permute-start.4) | collective-permute-done | bytes 2097184 | tf_op jit(solution)/shard_map/ppermute | solution.py:12
  346.1 43.5 %collective-permute-done.5 = f32[2,2,64,2048]{3,2,1,0:T(8,128)} collective-permute-done((f32[2,2,64,2048]{3,2,1,0:T(8,128)S(1)}, f32[2,2,64,2048]{3,2,1,0:T(8,128)}, u32[]{:S(2)}, u32[]{:S(2)}) %collective-permute-start.5) | collective-permute-done | bytes 2097184 | tf_op jit(solution)/shard_map/ppermute | solution.py:12
  389.5 6.3 multiply_subtract_fusion.4
  398.6 46.0 %collective-permute-done.6 = f32[2,2,64,2048]{3,2,1,0:T(8,128)S(1)} collective-permute-done((f32[2,2,64,2048]{3,2,1,0:T(8,128)}, f32[2,2,64,2048]{3,2,1,0:T(8,128)S(1)}, u32[]{:S(2)}, u32[]{:S(2)}) %collective-permute-start.6) | collective-permute-done | bytes 2097184 | tf_op jit(solution)/shard_map/ppermute | solution.py:12
  444.6 42.7 %collective-permute-done.7 = f32[2,2,64,2048]{3,2,1,0:T(8,128)} collective-permute-done((f32[2,2,64,2048]{3,2,1,0:T(8,128)}, f32[2,2,64,2048]{3,2,1,0:T(8,128)}, u32[]{:S(2)}, u32[]{:S(2)}) %collective-permute-start.7) | collective-permute-done | bytes 2097184 | tf_op jit(solution)/shard_map/ppermute | solution.py:12
  487.3 6.3 multiply_subtract_fusion.2
  498.4 6.9 fusion.72
  508.4 6.3 fusion.70
  518.9 5.1 add_bitcast_fusion
  524.0 6.8 fusion.3
  530.8 7.0 fusion.1
  537.8 6.6 fusion.9
  552.4 10.0 %fusion.12 = f32[2,2,64,32,64]{4,2,3,1,0:T(8,128)S(1)} fusion(f32[2,2,64,32,64]{4,2,3,1,0:T(8,128)} %fusion.1, f32[2,2,64,32,64]{4,3,2,1,0:T(8,128)} %copy-done.2), kind=kOutput, calls=%fused_computation.13 | convolution fusion | flops 403234816 | bytes 6291456 | tf_op jit(solution)/shard_map/...kb,bl->...kl/dot_general | solution.py:40
  566.8 5.0 reshape.347
  588.6 5.2 multiply_add_fusion.1
  593.8 5.6 multiply_add_fusion
  613.6 6.0 subtract_bitcast_fusion.1
  627.4 24.2 %collective-permute-done.9 = f32[2,64,2048]{2,1,0:T(8,128)} collective-permute-done((f32[2,64,2048]{2,1,0:T(8,128)S(1)}, f32[2,64,2048]{2,1,0:T(8,128)}, u32[]{:S(2)}, u32[]{:S(2)}) %collective-permute-start.9) | collective-permute-done | bytes 1048608 | tf_op jit(solution)/shard_map/ppermute | solution.py:12
  651.6 19.2 %collective-permute-done.8 = f32[2,64,2048]{2,1,0:T(8,128)} collective-permute-done((f32[2,64,2048]{2,1,0:T(8,128)}, f32[2,64,2048]{2,1,0:T(8,128)}, u32[]{:S(2)}, u32[]{:S(2)}) %collective-permute-start.8) | collective-permute-done | bytes 1048608 | tf_op jit(solution)/shard_map/ppermute | solution.py:12
  678.6 24.1 %collective-permute-done.11 = f32[2,64,2048]{2,1,0:T(8,128)S(1)} collective-permute-done((f32[2,64,2048]{2,1,0:T(8,128)S(1)}, f32[2,64,2048]{2,1,0:T(8,128)S(1)}, u32[]{:S(2)}, u32[]{:S(2)}) %collective-permute-start.11) | collective-permute-done | bytes 1048608 | tf_op jit(solution)/shard_map/ppermute | solution.py:12
  703.7 17.3 %collective-permute-done.10 = f32[2,64,2048]{2,1,0:T(8,128)} collective-permute-done((f32[2,64,2048]{2,1,0:T(8,128)}, f32[2,64,2048]{2,1,0:T(8,128)}, u32[]{:S(2)}, u32[]{:S(2)}) %collective-permute-start.10) | collective-permute-done | bytes 1048608 | tf_op jit(solution)/shard_map/ppermute | solution.py:12
  727.7 24.2 %collective-permute-done.13 = f32[2,64,2048]{2,1,0:T(8,128)} collective-permute-done((f32[2,64,2048]{2,1,0:T(8,128)S(1)}, f32[2,64,2048]{2,1,0:T(8,128)}, u32[]{:S(2)}, u32[]{:S(2)}) %collective-permute-start.13) | collective-permute-done | bytes 1048608 | tf_op jit(solution)/shard_map/ppermute | solution.py:12
  751.9 17.3 %collective-permute-done.12 = f32[2,64,2048]{2,1,0:T(8,128)} collective-permute-done((f32[2,64,2048]{2,1,0:T(8,128)}, f32[2,64,2048]{2,1,0:T(8,128)}, u32[]{:S(2)}, u32[]{:S(2)}) %collective-permute-start.12) | collective-permute-done | bytes 1048608 | tf_op jit(solution)/shard_map/ppermute | solution.py:12
  775.7 24.0 %collective-permute-done.15 = f32[2,64,2048]{2,1,0:T(8,128)S(1)} collective-permute-done((f32[2,64,2048]{2,1,0:T(8,128)S(1)}, f32[2,64,2048]{2,1,0:T(8,128)S(1)}, u32[]{:S(2)}, u32[]{:S(2)}) %collective-permute-start.15) | collective-permute-done | bytes 1048608 | tf_op jit(solution)/shard_map/ppermute | solution.py:12
  799.7 16.4 %collective-permute-done.14 = f32[2,64,2048]{2,1,0:T(8,128)S(1)} collective-permute-done((f32[2,64,2048]{2,1,0:T(8,128)S(1)}, f32[2,64,2048]{2,1,0:T(8,128)S(1)}, u32[]{:S(2)}, u32[]{:S(2)}) %collective-permute-start.14) | collective-permute-done | bytes 1048608 | tf_op jit(solution)/shard_map/ppermute | solution.py:12
  (86 shorter events, 110.6 us)
Async XLA Ops:
  6.5 1.9 copy-start
  6.5 85.7 %reduce-scatter.2.cloned.1.call-start = ((), (), s32[]{:S(2)}) async-start(), calls=%async_computation.1 | async-start | bytes 14155776 | tf_op jit(solution)/shard_map/reduce_scatter | solution.py:172
  19.9 74.8 %copy-start.14 = (bf16[64,2048]{1,0:T(8,128)(2,1)S(1)}, bf16[64,2048]{1,0:T(8,128)(2,1)}, u32[]{:S(2)}) copy-start(bf16[64,2048]{1,0:T(8,128)(2,1)} %param.5) | copy-start | bytes 786436
  93.8 0.9 copy-start.11
  96.7 49.9 %collective-permute-start = (f32[2,2,64,2048]{3,2,1,0:T(8,128)}, f32[2,2,64,2048]{3,2,1,0:T(8,128)}, u32[]{:S(2)}, u32[]{:S(2)}) collective-permute-start(f32[2,2,64,2048]{3,2,1,0:T(8,128)} %get-tuple-element.32), channel_id=1, source_target_pairs={{0,64},{8,72},{16,80},{24,88},{32,96},{40,104},{48,112},{56,120},{... | collective-permute-start | bytes 6291464 | tf_op jit(solution)/shard_map/ppermute | solution.py:12
  100.1 91.5 %collective-permute-start.1 = (f32[2,2,64,2048]{3,2,1,0:T(8,128)S(1)}, f32[2,2,64,2048]{3,2,1,0:T(8,128)}, u32[]{:S(2)}, u32[]{:S(2)}) collective-permute-start(f32[2,2,64,2048]{3,2,1,0:T(8,128)S(1)} %get-tuple-element.31), channel_id=1, source_target_pairs={{0,64},{8,72},{16,80},{24,88},{32,96},{40,104},{48,112},{56,120},{... | collective-permute-start | bytes 6291464 | tf_op jit(solution)/shard_map/ppermute | solution.py:12
  196.3 48.8 %copy-start.9 = (f32[2,2,64,2048]{3,2,1,0:T(8,128)}, f32[2,2,64,2048]{3,2,1,0:T(8,128)S(1)}, u32[]{:S(2)}) copy-start(f32[2,2,64,2048]{3,2,1,0:T(8,128)S(1)} %get-tuple-element.25) | copy-start | bytes 6291460
  196.4 48.8 %collective-permute-start.2 = (f32[2,2,64,2048]{3,2,1,0:T(8,128)}, f32[2,2,64,2048]{3,2,1,0:T(8,128)}, u32[]{:S(2)}, u32[]{:S(2)}) collective-permute-start(f32[2,2,64,2048]{3,2,1,0:T(8,128)} %get-tuple-element.26), channel_id=1, source_target_pairs={{0,32},{8,40},{16,48},{24,56},{32,0},{40,8},{48,16},{56,24},{64,96... | collective-permute-start | bytes 6291464 | tf_op jit(solution)/shard_map/ppermute | solution.py:12
  198.3 91.2 %collective-permute-start.3 = (f32[2,2,64,2048]{3,2,1,0:T(8,128)S(1)}, f32[2,2,64,2048]{3,2,1,0:T(8,128)}, u32[]{:S(2)}, u32[]{:S(2)}) collective-permute-start(f32[2,2,64,2048]{3,2,1,0:T(8,128)S(1)} %get-tuple-element.25), channel_id=1, source_target_pairs={{0,32},{8,40},{16,48},{24,56},{32,0},{40,8},{48,16},{56,24},{64,96... | collective-permute-start | bytes 6291464 | tf_op jit(solution)/shard_map/ppermute | solution.py:12
  295.7 50.4 %collective-permute-start.4 = (f32[2,2,64,2048]{3,2,1,0:T(8,128)}, f32[2,2,64,2048]{3,2,1,0:T(8,128)}, u32[]{:S(2)}, u32[]{:S(2)}) collective-permute-start(f32[2,2,64,2048]{3,2,1,0:T(8,128)} %get-tuple-element.24), channel_id=1, source_target_pairs={{0,16},{8,24},{16,0},{24,8},{32,48},{40,56},{48,32},{56,40},{64,80... | collective-permute-start | bytes 6291464 | tf_op jit(solution)/shard_map/ppermute | solution.py:12
  298.8 90.7 %collective-permute-start.5 = (f32[2,2,64,2048]{3,2,1,0:T(8,128)S(1)}, f32[2,2,64,2048]{3,2,1,0:T(8,128)}, u32[]{:S(2)}, u32[]{:S(2)}) collective-permute-start(f32[2,2,64,2048]{3,2,1,0:T(8,128)S(1)} %get-tuple-element.23), channel_id=1, source_target_pairs={{0,16},{8,24},{16,0},{24,8},{32,48},{40,56},{48,32},{56,40},{64,80... | collective-permute-start | bytes 6291464 | tf_op jit(solution)/shard_map/ppermute | solution.py:12
  395.8 48.8 %collective-permute-start.6 = (f32[2,2,64,2048]{3,2,1,0:T(8,128)}, f32[2,2,64,2048]{3,2,1,0:T(8,128)S(1)}, u32[]{:S(2)}, u32[]{:S(2)}) collective-permute-start(f32[2,2,64,2048]{3,2,1,0:T(8,128)} %get-tuple-element.22), channel_id=1, source_target_pairs={{0,8},{8,0},{16,24},{24,16},{32,40},{40,32},{48,56},{56,48},{64,72... | collective-permute-start | bytes 6291464 | tf_op jit(solution)/shard_map/ppermute | solution.py:12
  397.2 90.1 %collective-permute-start.7 = (f32[2,2,64,2048]{3,2,1,0:T(8,128)}, f32[2,2,64,2048]{3,2,1,0:T(8,128)}, u32[]{:S(2)}, u32[]{:S(2)}) collective-permute-start(f32[2,2,64,2048]{3,2,1,0:T(8,128)} %get-tuple-element.21), channel_id=1, source_target_pairs={{0,8},{8,0},{16,24},{24,16},{32,40},{40,32},{48,56},{56,48},{64,72... | collective-permute-start | bytes 6291464 | tf_op jit(solution)/shard_map/ppermute | solution.py:12
  444.6 42.7 %copy-start.12 = (f32[2,2,64,2048]{3,2,1,0:T(8,128)}, f32[2,2,64,2048]{3,2,1,0:T(8,128)S(1)}, u32[]{:S(2)}) copy-start(f32[2,2,64,2048]{3,2,1,0:T(8,128)S(1)} %collective-permute-done.6) | copy-start | bytes 6291460
  508.4 6.3 copy-start.4
  508.4 6.3 copy-start.6
  514.7 4.1 copy-start.3
  524.0 13.8 %copy-start.2 = (f32[2,2,64,32,64]{4,3,2,1,0:T(8,128)}, f32[2,2,64,32,64]{4,3,2,1,0:T(8,128)S(1)}, u32[]{:S(2)}) copy-start(f32[2,2,64,32,64]{4,3,2,1,0:T(8,128)S(1)} %get-tuple-element.17) | copy-start | bytes 6291460
  587.2 1.4 copy-start.5
  588.6 5.2 copy-start.8
  625.3 26.3 %collective-permute-start.9 = (f32[2,64,2048]{2,1,0:T(8,128)S(1)}, f32[2,64,2048]{2,1,0:T(8,128)}, u32[]{:S(2)}, u32[]{:S(2)}) collective-permute-start(f32[2,64,2048]{2,1,0:T(8,128)S(1)} %multiply_subtract_fusion.11), channel_id=1, source_target_pairs={{0,8},{8,0},{16,24},{24,16},{32,40},{40,32},{48,56},{56,48},{64,72... | collective-permute-start | bytes 3145736 | tf_op jit(solution)/shard_map/ppermute | solution.py:12
  626.4 44.3 %collective-permute-start.8 = (f32[2,64,2048]{2,1,0:T(8,128)}, f32[2,64,2048]{2,1,0:T(8,128)}, u32[]{:S(2)}, u32[]{:S(2)}) collective-permute-start(f32[2,64,2048]{2,1,0:T(8,128)} %get-tuple-element.14), channel_id=1, source_target_pairs={{0,8},{8,0},{16,24},{24,16},{32,40},{40,32},{48,56},{56,48},{64,72... | collective-permute-start | bytes 3145736 | tf_op jit(solution)/shard_map/ppermute | solution.py:12
  673.9 1.0 copy-start.7
  675.0 27.7 %copy-start.10 = (f32[2,64,2048]{2,1,0:T(8,128)}, f32[2,64,2048]{2,1,0:T(8,128)S(1)}, u32[]{:S(2)}) copy-start(f32[2,64,2048]{2,1,0:T(8,128)S(1)} %multiply_subtract_fusion.10) | copy-start | bytes 3145732
  675.0 27.7 %collective-permute-start.11 = (f32[2,64,2048]{2,1,0:T(8,128)S(1)}, f32[2,64,2048]{2,1,0:T(8,128)S(1)}, u32[]{:S(2)}, u32[]{:S(2)}) collective-permute-start(f32[2,64,2048]{2,1,0:T(8,128)S(1)} %multiply_subtract_fusion.10), channel_id=1, source_target_pairs={{0,16},{8,24},{16,0},{24,8},{32,48},{40,56},{48,32},{56,40},{64,80... | collective-permute-start | bytes 3145736 | tf_op jit(solution)/shard_map/ppermute | solution.py:12
  677.4 43.6 %collective-permute-start.10 = (f32[2,64,2048]{2,1,0:T(8,128)}, f32[2,64,2048]{2,1,0:T(8,128)}, u32[]{:S(2)}, u32[]{:S(2)}) collective-permute-start(f32[2,64,2048]{2,1,0:T(8,128)} %get-tuple-element.11), channel_id=1, source_target_pairs={{0,16},{8,24},{16,0},{24,8},{32,48},{40,56},{48,32},{56,40},{64,80... | collective-permute-start | bytes 3145736 | tf_op jit(solution)/shard_map/ppermute | solution.py:12
  702.7 1.0 copy-start.13
  725.6 26.3 %collective-permute-start.13 = (f32[2,64,2048]{2,1,0:T(8,128)S(1)}, f32[2,64,2048]{2,1,0:T(8,128)}, u32[]{:S(2)}, u32[]{:S(2)}) collective-permute-start(f32[2,64,2048]{2,1,0:T(8,128)S(1)} %multiply_subtract_fusion.9), channel_id=1, source_target_pairs={{0,32},{8,40},{16,48},{24,56},{32,0},{40,8},{48,16},{56,24},{64,96... | collective-permute-start | bytes 3145736 | tf_op jit(solution)/shard_map/ppermute | solution.py:12
  726.3 42.9 %collective-permute-start.12 = (f32[2,64,2048]{2,1,0:T(8,128)}, f32[2,64,2048]{2,1,0:T(8,128)}, u32[]{:S(2)}, u32[]{:S(2)}) collective-permute-start(f32[2,64,2048]{2,1,0:T(8,128)} %get-tuple-element.8), channel_id=1, source_target_pairs={{0,32},{8,40},{16,48},{24,56},{32,0},{40,8},{48,16},{56,24},{64,96... | collective-permute-start | bytes 3145736 | tf_op jit(solution)/shard_map/ppermute | solution.py:12
  772.0 27.7 %collective-permute-start.15 = (f32[2,64,2048]{2,1,0:T(8,128)S(1)}, f32[2,64,2048]{2,1,0:T(8,128)S(1)}, u32[]{:S(2)}, u32[]{:S(2)}) collective-permute-start(f32[2,64,2048]{2,1,0:T(8,128)S(1)} %multiply_subtract_fusion.8), channel_id=1, source_target_pairs={{0,64},{8,72},{16,80},{24,88},{32,96},{40,104},{48,112},{56,120},{... | collective-permute-start | bytes 3145736 | tf_op jit(solution)/shard_map/ppermute | solution.py:12
  774.0 42.1 %collective-permute-start.14 = (f32[2,64,2048]{2,1,0:T(8,128)S(1)}, f32[2,64,2048]{2,1,0:T(8,128)S(1)}, u32[]{:S(2)}, u32[]{:S(2)}) collective-permute-start(f32[2,64,2048]{2,1,0:T(8,128)S(1)} %get-tuple-element.5), channel_id=1, source_target_pairs={{0,64},{8,72},{16,80},{24,88},{32,96},{40,104},{48,112},{56,120},{... | collective-permute-start | bytes 3145736 | tf_op jit(solution)/shard_map/ppermute | solution.py:12
  775.7 42.8 %copy-start.1 = (bf16[3,1024,512]{2,1,0:T(8,128)(2,1)S(1)}, bf16[3,1024,512]{2,1,0:T(8,128)(2,1)}, u32[]{:S(2)}) copy-start(bf16[3,1024,512]{2,1,0:T(8,128)(2,1)} %param.4) | copy-start | bytes 9437188
Sparse Core Ops, SparseCore 0:
  20.0 72.2 reduce-scatter.1
where the time goes:
time: 833 us; the launch traced here: 826 us
  waiting for transfers between devices  600 us (72%)
  matrix products  102 us (12%)
  other arithmetic  46.7 us (6%)
  local copies, waits for them, and re-layouts  39.3 us (5%)
  starting transfers between devices  22.7 us (3%)
  between operations  14.6 us (2%)
    ppermute x16, waiting for transfers between devices, swapped(): lax.ppermute(value, axis, [(i, i ^ 1 << apart) for i in range(lax.axis_si...  528 us
    reduce_scatter x1, waiting for transfers between devices, per_device(): lax.psum_scatter(jnp.einsum('td,jdc->cjt', hidden_in, projection, preferr...  72.3 us
    dot_general x4, matrix products, complex_product(): jnp.einsum(form, real_part, sine, precision=highest)  26.7 us
    sub x9, other arithmetic, rotate(): imag_part * cosine - sign_value * real_part * sine  26.1 us
    dot_general x4, matrix products, complex_product(): jnp.einsum(form, real_part, cosine, precision=highest)  23.4 us
    ppermute x16, starting transfers between devices, swapped(): lax.ppermute(value, axis, [(i, i ^ 1 << apart) for i in range(lax.axis_si...  22.7 us
    dot_general x4, matrix products, complex_product(): jnp.einsum(form, imag_part, cosine, precision=highest)  22.3 us
    dot_general x4, matrix products, complex_product(): jnp.einsum(form, imag_part, sine, precision=highest)  18.6 us
  transfers between devices with their start and end apart: 17, of which 17 were waited for; matrix products, arithmetic and copies ran while one was open for 0% of the time, Pallas kernels for 0%

commit v1 on v0

v1 whole, which is shorter than its diff:
```python
import jax
import jax.numpy as jnp
import numpy as np
from jax import lax
from jax.sharding import PartitionSpec as P

ROWS, COLS = 256, 128
HIGH = lax.Precision.HIGH


def transform_tables():
    total = ROWS * COLS
    counter = np.arange(ROWS)
    first = 2.0 * np.pi * ((counter[:, None] * (4 * counter[None, :] + 1)) % (4 * ROWS)) / (4 * ROWS)
    inner = np.arange(COLS)
    twist = 2.0 * np.pi * (inner[None, :] * (4 * counter[:, None] + 1)) / (4 * total)
    second = 2.0 * np.pi * ((inner[:, None] * inner[None, :]) % COLS) / COLS
    return first, twist, second


def forward(signal, tables):
    first, twist, second = tables
    cos1, sin1 = np.float32(np.cos(first.T)), np.float32(np.sin(first.T))
    cosw, sinw = np.float32(np.cos(twist)), np.float32(np.sin(twist))
    cos2, sin2 = np.float32(np.cos(second)), np.float32(np.sin(second))
    real = jnp.einsum("kj,cjb->ckb", cos1, signal, precision=HIGH)
    imag = -jnp.einsum("kj,cjb->ckb", sin1, signal, precision=HIGH)
    real, imag = real * cosw + imag * sinw, imag * cosw - real * sinw
    both = jnp.concatenate([real, imag], axis=-1)
    mix = np.block([[cos2, -sin2], [sin2, cos2]])
    both = jnp.einsum("ckb,bl->ckl", both, mix, precision=HIGH)
    return both[..., :COLS], both[..., COLS:]


def backward(real, imag, tables):
    first, twist, second = tables
    cosw, sinw = np.float32(np.cos(twist)), np.float32(np.sin(twist))
    cos2, sin2 = np.float32(np.cos(second)), np.float32(np.sin(second))
    both = jnp.concatenate([real, imag], axis=-1)
    mix = np.block([[cos2, sin2], [-sin2, cos2]])
    both = jnp.einsum("ckb,bl->ckl", both, mix, precision=HIGH)
    real, imag = both[..., :COLS], both[..., COLS:]
    real, imag = real * cosw - imag * sinw, imag * cosw + real * sinw
    both = jnp.concatenate([real, imag], axis=1)
    last = np.float32(np.concatenate([np.cos(first), -np.sin(first)], axis=1) / (ROWS * COLS))
    return jnp.einsum("jk,ckb->cjb", last, both, precision=HIGH)


def to_channels(block):
    blocks = lax.axis_size("seq")
    block = block.reshape(blocks, -1, block.shape[-1])
    moved = lax.all_to_all(block, "seq", 0, 0, tiled=False)
    moved = jnp.swapaxes(moved, 0, 1)
    return moved.reshape(moved.shape[0], ROWS, COLS)


def to_positions(whole):
    blocks = lax.axis_size("seq")
    whole = whole.reshape(whole.shape[0], blocks, -1)
    moved = lax.all_to_all(jnp.swapaxes(whole, 0, 1), "seq", 0, 0, tiled=False)
    return moved.reshape(-1, moved.shape[-1])


def per_device(hidden_in, projection, filter_taps):
    tables = transform_tables()
    taps = to_channels(filter_taps).astype(jnp.float32)
    filter_real, filter_imag = forward(taps, tables)
    projected = lax.psum_scatter(
        jnp.einsum("td,jdc->cjt", hidden_in, projection, preferred_element_type=jnp.float32),
        "chan",
        scatter_dimension=0,
        tiled=True,
    ).astype(jnp.bfloat16)
    gating = projected[:, 0]
    mixed = (projected[:, 1].astype(jnp.float32) * projected[:, 2].astype(jnp.float32)).astype(
        jnp.bfloat16
    )
    real, imag = forward(to_channels(mixed).astype(jnp.float32), tables)
    real, imag = (
        real * filter_real - imag * filter_imag,
        real * filter_imag + imag * filter_real,
    )
    convolved = to_positions(backward(real, imag, tables))
    return (gating.astype(jnp.float32) * convolved).astype(jnp.bfloat16)


def solution(mesh):
    placed = (P("seq", "chan"), P(None, "chan", None), P("chan", "seq"))
    return jax.shard_map(
        per_device, mesh=mesh, in_specs=placed, out_specs=P("chan", "seq"), check_vma=False
    )
```

time: 833 us -> 154 us (0.18)
  the two profiles are of different devices: /device:TPU:8 before, /device:TPU:0 now
where the time goes in v1:
time: 154 us; the launch traced here: 152 us
  waiting for transfers between devices  56.6 us (37%)
  blocking collectives  29.8 us (19%)
  matrix products  23.2 us (15%)
  local copies, waits for them, and re-layouts  16.2 us (11%)
  between operations  13.6 us (9%)
  starting transfers between devices  6.94 us (5%)
  other arithmetic  5.7 us (4%)
    reduce_scatter x1, waiting for transfers between devices, per_device(): lax.psum_scatter(jnp.einsum('td,jdc->cjt', hidden_in, projection, preferr...  50.8 us
    all_to_all x1, blocking collectives, to_channels(): moved = lax.all_to_all(block, 'seq', 0, 0, tiled=False)  16.5 us
    all_to_all x1, blocking collectives, to_positions(): moved = lax.all_to_all(jnp.swapaxes(whole, 0, 1), 'seq', 0, 0, tiled=False)  13.4 us
    dot_general x1, matrix products, per_device(): jnp.einsum('td,jdc->cjt', hidden_in, projection, preferred_element_type=j...  11.4 us
    all_to_all x1, starting transfers between devices, to_channels(): moved = lax.all_to_all(block, 'seq', 0, 0, tiled=False)  6.93 us
    all_to_all x1, waiting for transfers between devices, to_channels(): moved = lax.all_to_all(block, 'seq', 0, 0, tiled=False)  5.85 us
    dot_general x2, matrix products, forward(): both = jnp.einsum('ckb,bl->ckl', both, mix, precision=HIGH)  4.43 us
  transfers between devices with their start and end apart: 2, of which 2 were waited for; matrix products, arithmetic and copies ran while one was open for 7% of the time, Pallas kernels for 0%

profile of v1, /device:TPU:0, one launch (start us, length us, event | category | flops | bytes accessed | tf_op | source)
XLA Modules:
  0.0 152.0 jit_solution(14584630660781997847)
XLA Ops:
  6.5 1.9 %copy-done = bf16[3,1024,512]{2,1,0:T(8,128)(2,1)S(1)} copy-done((bf16[3,1024,512]{2,1,0:T(8,128)(2,1)S(1)}, bf16[3,1024,512]{2,1,0:T(8,128)(2,1)}, u32[]{:S(2)}) %copy-start) | copy-done | bytes 3145752
  8.4 11.4 %convolution_bitcast_fusion = f32[512,3,2048]{2,0,1:T(8,128)} fusion(bf16[3,1024,512]{2,1,0:T(8,128)(2,1)S(1)} %copy-done, bf16[2048,1024]{1,0:T(8,128)(2,1)} %param.17), kind=kOutput, calls=%fused_computation | convolution fusion | flops 6442450944 | bytes 19922944 | tf_op jit(solution)/shard_map/td,jdc->cjt/dot_general | solution.py:69
  19.8 1.1 reshape.31
  20.9 16.5 %all_to_all.15 = bf16[16,4,2048]{2,1,0:T(4,128)(2,1)S(1)} all-to-all(bf16[16,4,2048]{2,1,0:T(4,128)(2,1)S(1)} %reshape.31), channel_id=1, replica_groups=mesh['seq'=16,'chan'=8] {'seq'}, dimensions={0} | all-to-all | bytes 524288 | tf_op jit(solution)/shard_map/all_to_all | solution.py:52
  37.4 0.1 copy.43
  37.5 0.8 reshape.32
  38.3 1.1 copy.44
  39.4 1.3 fusion.22
  40.7 1.3 fusion.23
  42.0 2.0 %add_bitcast_fusion = (f32[4,256,128]{1,2,0:T(8,128)}, f32[4,256,128]{1,2,0:T(8,128)}) fusion(f32[256,4,128]{0,2,1:T(8,128)S(1)} %bitcast.53, f32[256,4,128]{0,2,1:T(8,128)S(1)} %bitcast.54, f32[256,128]{0,1:T(8,128)} %constant.17.clone, f32[256,128]{0,1:T(8,128)S(1)} %copy-done.3), kind=kLoop, calls=%fused_computation.24 | loop fusion | flops 917504 | bytes 2359296 | tf_op jit(solution)/shard_map/add | solution.py:28
  44.0 50.8 %reduce-scatter.2.cloned.1.call-done = f32[64,3,2048]{2,0,1:T(8,128)} async-done(((f32[512,3,2048]{2,0,1:T(8,128)}), f32[64,3,2048]{2,0,1:T(8,128)}) %reduce-scatter.2.cloned.1.call-update) | async-done | bytes 1572880 | tf_op jit(solution)/shard_map/reduce_scatter | solution.py:68
  94.8 1.5 convert_element_type.31
  96.3 0.9 copy-done.2
  97.3 0.8 convert_element_type.37
  98.1 6.9 %all-to-all-start = ((bf16[16,4,2048]{2,1,0:T(4,128)(2,1)}), bf16[16,4,2048]{2,1,0:T(4,128)(2,1)S(1)}, u32[]{:S(2)}, u32[]{:S(2)}) async-start(bf16[16,4,2048]{2,1,0:T(4,128)(2,1)} %convert_element_type.37), calls=%async_computation.1 | async-start | bytes 524288 | tf_op jit(solution)/shard_map/all_to_all | solution.py:52
  105.1 2.8 %fusion.6 = f32[4,256,256]{1,2,0:T(8,128)} fusion(f32[256,256,1]{0,1,2:T(8,128)} %constant.23, f32[4,256,128]{1,2,0:T(8,128)} %get-tuple-element.12, f32[4,256,128]{1,2,0:T(8,128)} %get-tuple-element.11), kind=kOutput, calls=%fused_computation.10 | convolution fusion | flops 402915328 | bytes 2359296 | tf_op jit(solution)/shard_map/ckb,bl->ckl/dot_general | solution.py:31
  107.9 5.8 %all-to-all-done = bf16[16,4,2048]{2,1,0:T(4,128)(2,1)S(1)} async-done(((bf16[16,4,2048]{2,1,0:T(4,128)(2,1)}), bf16[16,4,2048]{2,1,0:T(4,128)(2,1)S(1)}, u32[]{:S(2)}, u32[]{:S(2)}) %all-to-all-start) | async-done | bytes 262176 | tf_op jit(solution)/shard_map/all_to_all | solution.py:52
  113.8 0.9 copy.39
  114.6 1.1 reshape.30
  115.7 1.4 convolution_bitcast_fusion.2
  117.1 1.4 multiply_add_fusion.2
  118.5 1.6 %fusion.2 = f32[4,256,256]{1,2,0:T(8,128)S(1)} fusion(f32[256,256,1]{0,1,2:T(8,128)} %constant.23, f32[4,256,128]{1,2,0:T(8,128)S(1)} %get-tuple-element.10, f32[4,256,128]{1,2,0:T(8,128)S(1)} %get-tuple-element.9), kind=kOutput, calls=%fused_computation.6 | convolution fusion | flops 402915328 | bytes 2359296 | tf_op jit(solution)/shard_map/ckb,bl->ckl/dot_general | solution.py:31
  120.2 0.1 multiply_subtract_fusion.1
  120.3 0.6 fusion.10
  121.0 0.1 multiply_subtract_fusion
  121.2 1.4 convolution_bitcast_fusion.1
  122.6 2.0 %copy.50 = f32[4,256,128]{2,1,0:T(8,128)} copy(f32[4,256,128]{1,2,0:T(8,128)} %convolution_bitcast_fusion.1) | data formatting | bytes 1048576 | tf_op jit(solution)/shard_map/jk,ckb->cjb/transpose | solution.py:46
  124.6 1.9 %reshape.33 = f32[4,16,2048]{2,1,0:T(8,128)} reshape(f32[4,256,128]{2,1,0:T(8,128)} %copy.50) | data formatting | bytes 1048576 | tf_op jit(solution)/shard_map/reshape | solution.py:59
  126.6 1.4 copy.51
  127.9 13.4 %all_to_all.16 = f32[16,4,2048]{2,1,0:T(4,128)} all-to-all(f32[16,4,2048]{2,1,0:T(4,128)S(1)} %copy.51), channel_id=1, replica_groups=mesh['seq'=16,'chan'=8] {'seq'}, dimensions={0} | all-to-all | bytes 1048576 | tf_op jit(solution)/shard_map/all_to_all | solution.py:60
  141.3 2.0 %reshape.34 = f32[64,2048]{1,0:T(8,128)} reshape(f32[16,4,2048]{2,1,0:T(4,128)} %all_to_all.16) | data formatting | bytes 1048576 | tf_op jit(solution)/shard_map/reshape | solution.py:61
  143.3 1.9 %fusion.17 = bf16[64,2048]{1,0:T(8,128)(2,1)} fusion(f32[64,2048]{1,0:T(8,128)} %reshape.34, bf16[64,3,2048]{2,0,1:T(8,128)(2,1)} %copy-done.2), kind=kLoop, calls=%fused_computation.22 | loop fusion | flops 393216 | bytes 1048576 | tf_op jit(solution)/shard_map/convert_element_type | solution.py:84
  (15 shorter events, 0.2 us)
Async XLA Ops:
  6.5 1.9 %copy-start = (bf16[3,1024,512]{2,1,0:T(8,128)(2,1)S(1)}, bf16[3,1024,512]{2,1,0:T(8,128)(2,1)}, u32[]{:S(2)}) copy-start(bf16[3,1024,512]{2,1,0:T(8,128)(2,1)} %param.18) | copy-start | bytes 9437188
  6.5 88.3 %reduce-scatter.2.cloned.1.call-start = ((), (), s32[]{:S(2)}) async-start(), calls=%async_computation.4 | async-start | bytes 14155776 | tf_op jit(solution)/shard_map/reduce_scatter | solution.py:68
  19.8 22.2 %copy-start.3 = (f32[256,128]{0,1:T(8,128)S(1)}, f32[256,128]{0,1:T(8,128)}, u32[]{:S(2)}) copy-start(f32[256,128]{0,1:T(8,128)} %constant.16.clone) | copy-start | bytes 393220
  96.3 0.9 copy-start.2
  98.1 15.6 %all-to-all-start = ((bf16[16,4,2048]{2,1,0:T(4,128)(2,1)}), bf16[16,4,2048]{2,1,0:T(4,128)(2,1)S(1)}, u32[]{:S(2)}, u32[]{:S(2)}) async-start(bf16[16,4,2048]{2,1,0:T(4,128)(2,1)} %convert_element_type.37), calls=%async_computation.1 | async-start | bytes 524288 | tf_op jit(solution)/shard_map/all_to_all | solution.py:52
  115.7 4.4 %copy-start.1 = (f32[4,256,256]{1,2,0:T(8,128)S(1)}, f32[4,256,256]{1,2,0:T(8,128)}, u32[]{:S(2)}) copy-start(f32[4,256,256]{1,2,0:T(8,128)} %fusion.6) | copy-start | bytes 3145732
  117.1 3.2 %copy-start.6 = (f32[256,256,1]{1,0,2:T(8,128)S(1)}, f32[256,256,1]{1,0,2:T(8,128)}, u32[]{:S(2)}) copy-start(f32[256,256,1]{1,0,2:T(8,128)} %constant.24) | copy-start | bytes 786436
  118.5 2.4 %copy-start.4 = (f32[256,128]{0,1:T(8,128)S(1)}, f32[256,128]{0,1:T(8,128)}, u32[]{:S(2)}) copy-start(f32[256,128]{0,1:T(8,128)} %constant.17.clone) | copy-start | bytes 393220
  120.1 1.0 copy-start.5
Sparse Core Ops, SparseCore 0:
  19.9 74.8 reduce-scatter.1

commit v2 on v1

v2 whole, which is shorter than its diff:
```python
import functools

import jax
import jax.numpy as jnp
import numpy as np
from jax import lax
from jax.experimental import pallas as pl
from jax.experimental.pallas import tpu as pltpu
from jax.sharding import PartitionSpec as P

ROWS, COLS = 256, 128
CHUNKS = 6
MIXES = 4
HALF = 1024
TILE = 256
BF16 = jnp.bfloat16
F32 = jnp.float32


def split_table(table):
    high = np.asarray(table, np.float32).astype(BF16)
    low = (np.asarray(table, np.float64) - high.astype(np.float64)).astype(np.float32).astype(BF16)
    return np.stack([high, low])


def transform_tables():
    total = ROWS * COLS
    counter = np.arange(ROWS)
    outer = 2.0 * np.pi * ((counter[:, None] * (4 * counter[None, :] + 1)) % (4 * ROWS)) / (4 * ROWS)
    inner = np.arange(COLS)
    twist = 2.0 * np.pi * (inner[None, :] * (4 * counter[:, None] + 1)) / (4 * total)
    second = 2.0 * np.pi * ((inner[:, None] * inner[None, :]) % COLS) / COLS
    first = np.concatenate([np.cos(outer.T), -np.sin(outer.T)], axis=0)
    last = np.concatenate([np.cos(outer), -np.sin(outer)], axis=1) / total
    cos2, sin2 = np.cos(second), np.sin(second)
    ahead = np.block([[cos2, -sin2], [sin2, cos2]])
    back = np.block([[cos2, sin2], [-sin2, cos2]])
    turn = np.stack([np.cos(twist), -np.sin(twist)]).astype(np.float32)
    return (
        split_table(first),
        split_table(ahead),
        split_table(back),
        split_table(last),
        turn,
    )


def dot(left, right):
    return jnp.dot(left, right, preferred_element_type=F32)


def halves_of(value):
    high = value.astype(BF16)
    return high, (value - high.astype(F32)).astype(BF16)


def kernel(
    hidden_hbm, proj_hbm, taps_hbm, first_hbm, ahead_hbm, back_hbm, last_hbm, turn_hbm,
    out_hbm,
    hidden, proj, taps, first, ahead, back, last, turn,
    weights, own, core_out, core_in, ring_out, ring_in,
    relay, taps_out, taps_in, mixed_out, mixed_in, spectrum, conv_out, conv_in, gates, gated,
    load_sem, core_send, core_recv, ring_send, ring_recv,
    taps_send, taps_recv, mixed_send, mixed_recv, conv_send, conv_recv, store_sem,
):
    seq = lax.axis_index("seq")
    chan = lax.axis_index("chan")
    blocks = lax.axis_size("seq")
    y = chan // 2
    core = lax.rem(chan, 2)
    partner = {"chan": y * 2 + 1 - core}
    right = {"chan": lax.rem(y + 1, 4) * 2 + core}
    left = {"chan": lax.rem(y + 3, 4) * 2 + core}

    loads = []

    def load(src, dst):
        copy = pltpu.make_async_copy(src, dst, load_sem.at[len(loads)])
        copy.start()
        loads.append(copy)
        return copy

    proj_loads = [None, load(proj_hbm.at[1], proj.at[1]), load(proj_hbm.at[2], proj.at[2])]
    hidden_loads = [
        load(hidden_hbm.at[pl.ds(n * HALF, HALF)], hidden.at[pl.ds(n * HALF, HALF)])
        for n in range(2)
    ]
    taps_load = load(taps_hbm, taps)
    proj_loads[0] = load(proj_hbm.at[0], proj.at[0])
    table_loads = [
        load(first_hbm, first),
        load(ahead_hbm, ahead),
        load(back_hbm, back),
        load(last_hbm, last),
        load(turn_hbm, turn),
    ]

    barrier = pltpu.get_barrier_semaphore()
    for near in (partner, right, left):
        pl.semaphore_signal(barrier, inc=1, device_id=near, device_id_type=pl.DeviceIdType.MESH)

    @pl.loop(1, blocks)
    def _(step):
        pl.semaphore_signal(
            barrier,
            inc=1,
            device_id={"seq": lax.rem(seq + step, blocks)},
            device_id_type=pl.DeviceIdType.MESH,
        )

    def remote(src, dst, send, recv, device):
        return pltpu.make_async_remote_copy(
            src_ref=src, dst_ref=dst, send_sem=send, recv_sem=recv,
            device_id=device, device_id_type=pl.DeviceIdType.MESH,
        )

    def exchange(src, dst, send, recv):
        pltpu.make_async_copy(src.at[seq], dst.at[seq], recv).start()

        @pl.loop(1, blocks)
        def _(step):
            peer = lax.rem(seq + step, blocks)
            remote(src.at[peer], dst.at[seq], send, recv, {"seq": peer}).start()

    def exchange_arrived(src, dst, recv):
        pltpu.make_async_copy(src, dst, recv).wait()

    def exchange_left(src, dst, send):
        count = blocks - 1
        pltpu.make_async_copy(src.at[pl.ds(0, count)], dst.at[pl.ds(0, count)], send).wait()

    def spread(block, part):
        for tile in range(HALF // COLS):
            relay[pl.ds((part * (HALF // COLS) + tile) * 16, 16), :] = block[
                :, tile * COLS : (tile + 1) * COLS
            ]

    def turn_weights(kind):
        proj_loads[kind].wait()
        for ahead_by in range(4):
            lane = pl.multiple_of(lax.rem(y + ahead_by, 4) * 128, 128)
            turned = proj[kind, :, pl.ds(lane, 128)].T
            for side in range(2):
                place = (1 - core if side == 0 else core) * 128 + 32 * ahead_by
                if kind == 0:
                    for part in range(2):
                        row = pl.multiple_of(place, 32)
                        weights[MIXES + part, pl.ds(row, 32), :] = turned[
                            side * 64 + 32 * part : side * 64 + 32 * part + 32
                        ]
                else:
                    for part in range(MIXES):
                        row = pl.multiple_of(place + 16 * (kind - 1), 16)
                        weights[part, pl.ds(row, 16), :] = turned[
                            side * 64 + 16 * part : side * 64 + 16 * part + 16
                        ]

    def core_copy(c, h):
        return remote(
            core_out.at[c, h], core_in.at[c, h], core_send.at[c, h], core_recv.at[c, h], partner
        )

    def ring_copy(c, kind):
        return remote(
            ring_out.at[c, kind], ring_in.at[c, kind], ring_send.at[c, kind],
            ring_recv.at[c, kind], right if kind % 2 == 0 else left,
        )

    def multiply(c):
        for h in range(2):
            if c == 0:
                hidden_loads[h].wait()

            @pl.loop(0, HALF // TILE)
            def _(n):
                rows = pl.multiple_of(h * HALF + n * TILE, TILE)
                product = lax.dot_general(
                    weights[c], hidden[pl.ds(rows, TILE), :],
                    (((1,), (1,)), ((), ())), preferred_element_type=F32,
                )
                lanes = pl.ds(pl.multiple_of(n * TILE, TILE), TILE)
                core_out[c, h, :, lanes] = product[:128].astype(BF16)
                own[c, h, :, lanes] = product[128:]

            core_copy(c, h).start()

    def combine(c):
        for h in range(2):
            core_copy(c, h).wait_recv()
            ring_out[c, h] = (own[c, h, 64:96] + core_in[c, h, 64:96].astype(F32)).astype(BF16)
            ring_copy(c, h).start()
            direct, later = (96, 32) if h == 0 else (32, 96)
            kind = 3 if h == 0 else 2
            ring_out[c, kind] = (
                own[c, h, direct : direct + 32] + core_in[c, h, direct : direct + 32].astype(F32)
            ).astype(BF16)
            ring_copy(c, kind).start()
            for row in (0, later):
                own[c, h, row : row + 32] = own[c, h, row : row + 32] + core_in[
                    c, h, row : row + 32
                ].astype(F32)

    def pass_on(c):
        for h in range(2):
            ring_copy(c, h).wait_recv()
            later = 32 if h == 0 else 96
            ring_out[c, 4 + h] = (
                own[c, h, later : later + 32] + ring_in[c, h].astype(F32)
            ).astype(BF16)
            ring_copy(c, 4 + h).start()

    def finish(c):
        for h in range(2):
            kinds = (3, 4) if h == 0 else (2, 5)
            total = own[c, h, 0:32]
            for kind in kinds:
                ring_copy(c, kind).wait_recv()
                total = total + ring_in[c, kind].astype(F32)
            if c >= MIXES:
                gates[pl.ds((c - MIXES) * 32, 32), pl.ds(h * HALF, HALF)] = total
            else:
                spread(total[:16] * total[16:], h)
        if c < MIXES:
            for peer in range(16):
                mixed_out[c, peer] = relay[pl.ds(peer, 16, stride=16), :].astype(BF16)
            exchange(mixed_out.at[c], mixed_in.at[c], mixed_send.at[c], mixed_recv.at[c])

    def transformed(signal):
        value = dot(first[0], signal) + dot(first[1], signal)
        real, imag = value[:ROWS], value[ROWS:]
        value = jnp.concatenate(
            [real * turn[0] - imag * turn[1], real * turn[1] + imag * turn[0]], axis=1
        )
        high, low = halves_of(value)
        return dot(high, ahead[0]) + dot(high, ahead[1]) + dot(low, ahead[0])

    def send_taps():
        taps_load.wait()
        for q in range(MIXES):
            for h in range(2):
                spread(taps[q * 16 : q * 16 + 16, h * HALF : (h + 1) * HALF].astype(F32), h)
            for peer in range(16):
                taps_out[peer, q] = relay[pl.ds(peer, 16, stride=16), :].astype(BF16)
        exchange(taps_out, taps_in, taps_send, taps_recv)

    def filter_spectra():
        exchange_arrived(taps_out, taps_in, taps_recv)
        for copy in table_loads:
            copy.wait()
        for q in range(MIXES):
            spectrum[q] = transformed(taps_in[:, q].reshape(ROWS, COLS))

    def convolve(q):
        exchange_arrived(mixed_out.at[q], mixed_in.at[q], mixed_recv.at[q])
        value = transformed(mixed_in[q].reshape(ROWS, COLS))
        real, imag = value[:, :COLS], value[:, COLS:]
        freal, fimag = spectrum[q, :, :COLS], spectrum[q, :, COLS:]
        value = jnp.concatenate(
            [real * freal - imag * fimag, real * fimag + imag * freal], axis=1
        )
        high, low = halves_of(value)
        value = dot(high, back[0]) + dot(high, back[1]) + dot(low, back[0])
        real, imag = value[:, :COLS], value[:, COLS:]
        value = jnp.concatenate(
            [real * turn[0] + imag * turn[1], imag * turn[0] - real * turn[1]], axis=0
        )
        high, low = halves_of(value)
        value = dot(last[0], high) + dot(last[0], low) + dot(last[1], high)
        conv_out[q] = value.reshape(16, 16, COLS)
        exchange(conv_out.at[q], conv_in.at[q], conv_send.at[q], conv_recv.at[q])

    def emit(q):
        exchange_arrived(conv_out.at[q], conv_in.at[q], conv_recv.at[q])
        relay[...] = conv_in[q].reshape(256, COLS)
        rows = pl.ds(q * 16, 16)
        for tile in range(16):
            lanes = pl.ds(tile * COLS, COLS)
            part = relay[pl.ds(tile, 16, stride=16), :]
            gated[rows, lanes] = (gates[rows, lanes] * part).astype(BF16)
        pltpu.make_async_copy(gated.at[rows], out_hbm.at[rows], store_sem.at[q]).start()

    turn_weights(1)
    turn_weights(2)
    pl.semaphore_wait(barrier, 3 + blocks - 1)
    multiply(0)
    send_taps()
    multiply(1)
    combine(0)
    turn_weights(0)
    multiply(2)
    pass_on(0)
    combine(1)
    filter_spectra()
    finish(0)
    multiply(3)
    pass_on(1)
    combine(2)
    finish(1)
    convolve(0)
    multiply(4)
    pass_on(2)
    combine(3)
    finish(2)
    convolve(1)
    multiply(5)
    pass_on(3)
    combine(4)
    finish(3)
    convolve(2)
    pass_on(4)
    combine(5)
    finish(4)
    convolve(3)
    pass_on(5)
    emit(0)
    emit(1)
    finish(5)
    emit(2)
    emit(3)

    for c in range(CHUNKS):
        for h in range(2):
            core_copy(c, h).wait_send()
        for kind in range(6):
            ring_copy(c, kind).wait_send()
    exchange_left(taps_out, taps_in, taps_send)
    for q in range(MIXES):
        exchange_left(mixed_out.at[q], mixed_in.at[q], mixed_send.at[q])
        exchange_left(conv_out.at[q], conv_in.at[q], conv_send.at[q])
        rows = pl.ds(q * 16, 16)
        pltpu.make_async_copy(gated.at[rows], out_hbm.at[rows], store_sem.at[q]).wait()


def per_device(hidden_in, projection, filter_taps):
    tables = transform_tables()
    blocks = lax.axis_size("seq")
    anywhere = pl.BlockSpec(memory_space=pl.ANY)
    dma = pltpu.SemaphoreType.DMA
    return pl.pallas_call(
        kernel,
        out_shape=jax.ShapeDtypeStruct(filter_taps.shape, BF16),
        in_specs=[anywhere] * (3 + len(tables)),
        out_specs=anywhere,
        scratch_shapes=[
            pltpu.VMEM(hidden_in.shape, BF16),
            pltpu.VMEM(projection.shape, BF16),
            pltpu.VMEM(filter_taps.shape, BF16),
        ]
        + [pltpu.VMEM(table.shape, table.dtype) for table in tables]
        + [
            pltpu.VMEM((CHUNKS, 256, hidden_in.shape[1]), BF16),
            pltpu.VMEM((CHUNKS, 2, 128, HALF), F32),
            pltpu.VMEM((CHUNKS, 2, 128, HALF), BF16),
            pltpu.VMEM((CHUNKS, 2, 128, HALF), BF16),
            pltpu.VMEM((CHUNKS, 6, 32, HALF), BF16),
            pltpu.VMEM((CHUNKS, 6, 32, HALF), BF16),
            pltpu.VMEM((256, COLS), F32),
            pltpu.VMEM((blocks, MIXES, 16, COLS), BF16),
            pltpu.VMEM((blocks, MIXES, 16, COLS), BF16),
            pltpu.VMEM((MIXES, blocks, 16, COLS), BF16),
            pltpu.VMEM((MIXES, blocks, 16, COLS), BF16),
            pltpu.VMEM((MIXES, ROWS, 2 * COLS), F32),
            pltpu.VMEM((MIXES, blocks, 16, COLS), F32),
            pltpu.VMEM((MIXES, blocks, 16, COLS), F32),
            pltpu.VMEM(filter_taps.shape, F32),
            pltpu.VMEM(filter_taps.shape, BF16),
            dma((11,)),
            dma((CHUNKS, 2)),
            dma((CHUNKS, 2)),
            dma((CHUNKS, 6)),
            dma((CHUNKS, 6)),
            dma(()),
            dma(()),
            dma((MIXES,)),
            dma((MIXES,)),
            dma((MIXES,)),
            dma((MIXES,)),
            dma((MIXES,)),
        ],
        compiler_params=pltpu.CompilerParams(
            collective_id=0, has_side_effects=True, vmem_limit_bytes=60 * 1024 * 1024
        ),
        cost_estimate=pl.CostEstimate(
            flops=7_000_000_000, bytes_accessed=8_000_000, transcendentals=0
        ),
    )(hidden_in, projection, filter_taps, *[jnp.asarray(table) for table in tables])


def solution(mesh):
    placed = (P("seq", "chan"), P(None, "chan", None), P("chan", "seq"))
    return jax.shard_map(
        per_device, mesh=mesh, in_specs=placed, out_specs=P("chan", "seq"), check_vma=False
    )
```

time: 154 us -> 60.8 us (0.39); the launches traced: 152 us -> 60.7 us
  Pallas kernels: 0 us -> 59 us
  waiting for transfers between devices: 56.6 us -> 0 us
  blocking collectives: 29.8 us -> 0 us
  matrix products: 23.2 us -> 0 us
  local copies, waits for them, and re-layouts: 16.2 us -> 1.67 us
  between operations: 13.6 us -> 0.01 us
  starting transfers between devices: 6.94 us -> 0 us
  other arithmetic: 5.7 us -> 0 us
    pallas_call x0 -> x1, Pallas kernels: none -> 59 us  [per_device(): pl.pallas_call(kernel, out_shape=jax.ShapeDtypeStruct(filter_taps.shape,...]
    reduce_scatter x1 -> x0, waiting for transfers between devices: 50.8 us -> none  [per_device(): lax.psum_scatter(jnp.einsum('td,jdc->cjt', hidden_in, projection, preferr...]
    all_to_all x2 -> x0, blocking collectives: 29.8 us -> none  [the longest x1 16.5 us: to_channels(): moved = lax.all_to_all(block, 'seq', 0, 0, tiled=False)]
    dot_general x7 -> x0, matrix products: 20.6 us -> none  [the longest x1 11.4 us: per_device(): jnp.einsum('td,jdc->cjt', hidden_in, projection, preferred_element_type=j...]
    reshape x6 -> x0, local copies, waits for them, and re-layouts: 8 us -> none  [the longest x3 2.98 us: to_channels(): return moved.reshape(moved.shape[0], ROWS, COLS)]
    all_to_all x1 -> x0, starting transfers between devices: 6.93 us -> none  [to_channels(): moved = lax.all_to_all(block, 'seq', 0, 0, tiled=False)]
    all_to_all x1 -> x0, waiting for transfers between devices: 5.85 us -> none  [to_channels(): moved = lax.all_to_all(block, 'seq', 0, 0, tiled=False)]
    transpose x4 -> x0, local copies, waits for them, and re-layouts: 4.42 us -> none  [the longest x1 2.04 us: backward(): return jnp.einsum('jk,ckb->cjb', last, both, precision=HIGH)]
  transfers between devices with their start and end apart: 2 -> 0, of which waited for: 2 -> 0; matrix products, arithmetic and copies ran while one was open for 7% -> 0% of each run, Pallas kernels for 0% -> 0%
where the time goes in v2:
time: 60.8 us; the launch traced here: 60.7 us
  Pallas kernels  59 us (97%)
  local copies, waits for them, and re-layouts  1.67 us (3%)
    pallas_call x1, Pallas kernels, per_device(): pl.pallas_call(kernel, out_shape=jax.ShapeDtypeStruct(filter_taps.shape,...  59 us
    unnamed x1, local copies, waits for them, and re-layouts  1.67 us

profile of v2, /device:TPU:0, one launch (start us, length us, event | category | flops | bytes accessed | tf_op | source)
XLA Modules:
  0.0 60.7 jit_solution(11099037697257896348)
XLA Ops:
  0.0 59.0 %shard_map.82 = bf16[64,2048]{1,0:T(8,128)(2,1)} custom-call(bf16[2048,1024]{1,0:T(8,128)(2,1)} %hidden_hbm.1, bf16[3,1024,512]{2,1,0:T(8,128)(2,1)} %proj_hbm.1, bf16[64,2048]{1,0:T(8,128)(2,1)} %taps_hbm.1, bf16[2,512,256]{2,1,0:T(8,128)(2,1)} %constant.10.clone.first_hbm, bf16[2,256,256]{2,1,0:T(8,128)(2,1)} %constant.11.clone.ahead_hbm, ...), custom_call_target="tpu_custom_call" | custom-call | flops 7000000000 | bytes 8000000 | tf_op jit(solution)/shard_map/pallas_call | solution.py:339
  59.0 1.7 %copy.10 = bf16[64,2048]{1,0:T(8,128)(2,1)} copy(bf16[64,2048]{1,0:T(8,128)(2,1)} %shard_map.82) | data formatting | bytes 524288

commit v3 on v2

--- a/solution.py
+++ b/solution.py
@@ -61,7 +61,7 @@
     weights, own, core_out, core_in, ring_out, ring_in,
     relay, taps_out, taps_in, mixed_out, mixed_in, spectrum, conv_out, conv_in, gates, gated,
     load_sem, core_send, core_recv, ring_send, ring_recv,
-    taps_send, taps_recv, mixed_send, mixed_recv, conv_send, conv_recv, store_sem,
+    taps_send, taps_recv, mixed_send, mixed_recv, conv_send, conv_recv, store_sem, near_sem, far_sem,
 ):
     seq = lax.axis_index("seq")
     chan = lax.axis_index("chan")
@@ -95,18 +95,22 @@
         load(turn_hbm, turn),
     ]
 
+    def signal(semaphore, device):
+        pl.semaphore_signal(
+            semaphore, inc=1, device_id=device, device_id_type=pl.DeviceIdType.MESH
+        )
+
+    side = 4
+    z, x = seq // side, lax.rem(seq, side)
+
+    def plane(by_z, by_x):
+        return {"seq": lax.rem(z + by_z, side) * side + lax.rem(x + by_x, side)}
+
+    around = [plane(0, 1), plane(0, side - 1), plane(1, 0), plane(side - 1, 0)]
+    across = [plane(0, 2), plane(2, 0)]
     barrier = pltpu.get_barrier_semaphore()
-    for near in (partner, right, left):
-        pl.semaphore_signal(barrier, inc=1, device_id=near, device_id_type=pl.DeviceIdType.MESH)
-
-    @pl.loop(1, blocks)
-    def _(step):
-        pl.semaphore_signal(
-            barrier,
-            inc=1,
-            device_id={"seq": lax.rem(seq + step, blocks)},
-            device_id_type=pl.DeviceIdType.MESH,
-        )
+    for near in [partner, right, left] + around:
+        signal(barrier, near)
 
     def remote(src, dst, send, recv, device):
         return pltpu.make_async_remote_copy(
@@ -115,19 +119,21 @@
         )
 
     def exchange(src, dst, send, recv):
-        pltpu.make_async_copy(src.at[seq], dst.at[seq], recv).start()
+        pltpu.make_async_copy(src(seq), dst(seq), recv).start()
 
         @pl.loop(1, blocks)
         def _(step):
             peer = lax.rem(seq + step, blocks)
-            remote(src.at[peer], dst.at[seq], send, recv, {"seq": peer}).start()
+            remote(src(peer), dst(seq), send, recv, {"seq": peer}).start()
 
     def exchange_arrived(src, dst, recv):
         pltpu.make_async_copy(src, dst, recv).wait()
 
-    def exchange_left(src, dst, send):
-        count = blocks - 1
+    def exchange_left(src, dst, send, count):
         pltpu.make_async_copy(src.at[pl.ds(0, count)], dst.at[pl.ds(0, count)], send).wait()
+
+    def rows_of(ref):
+        return lambda peer: ref.at[pl.ds(pl.multiple_of(peer * 16, 16), 16)]
 
     def spread(block, part):
         for tile in range(HALF // COLS):
@@ -170,35 +176,32 @@
         for h in range(2):
             if c == 0:
                 hidden_loads[h].wait()
-
-            @pl.loop(0, HALF // TILE)
-            def _(n):
-                rows = pl.multiple_of(h * HALF + n * TILE, TILE)
-                product = lax.dot_general(
-                    weights[c], hidden[pl.ds(rows, TILE), :],
-                    (((1,), (1,)), ((), ())), preferred_element_type=F32,
-                )
-                lanes = pl.ds(pl.multiple_of(n * TILE, TILE), TILE)
-                core_out[c, h, :, lanes] = product[:128].astype(BF16)
-                own[c, h, :, lanes] = product[128:]
-
+            product = lax.dot_general(
+                weights[c], hidden[h * HALF : (h + 1) * HALF],
+                (((1,), (1,)), ((), ())), preferred_element_type=F32,
+            )
+            core_out[c, h] = product[:128].astype(BF16)
+            own[c, h] = product[128:]
+
+    def core_go(c):
+        for h in range(2):
             core_copy(c, h).start()
 
     def combine(c):
+        def summed(h, row):
+            return own[c, h, row : row + 32] + core_in[c, h, row : row + 32].astype(F32)
+
         for h in range(2):
             core_copy(c, h).wait_recv()
-            ring_out[c, h] = (own[c, h, 64:96] + core_in[c, h, 64:96].astype(F32)).astype(BF16)
+            ring_out[c, h] = summed(h, 64).astype(BF16)
             ring_copy(c, h).start()
-            direct, later = (96, 32) if h == 0 else (32, 96)
+        for h in range(2):
             kind = 3 if h == 0 else 2
-            ring_out[c, kind] = (
-                own[c, h, direct : direct + 32] + core_in[c, h, direct : direct + 32].astype(F32)
-            ).astype(BF16)
+            ring_out[c, kind] = summed(h, 96 if h == 0 else 32).astype(BF16)
             ring_copy(c, kind).start()
-            for row in (0, later):
-                own[c, h, row : row + 32] = own[c, h, row : row + 32] + core_in[
-                    c, h, row : row + 32
-                ].astype(F32)
+        for h in range(2):
+            for row in (32 if h == 0 else 96, 0):
+                own[c, h, row : row + 32] = summed(h, row)
 
     def pass_on(c):
         for h in range(2):
@@ -222,37 +225,48 @@
                 spread(total[:16] * total[16:], h)
         if c < MIXES:
             for peer in range(16):
-                mixed_out[c, peer] = relay[pl.ds(peer, 16, stride=16), :].astype(BF16)
-            exchange(mixed_out.at[c], mixed_in.at[c], mixed_send.at[c], mixed_recv.at[c])
-
-    def transformed(signal):
-        value = dot(first[0], signal) + dot(first[1], signal)
-        real, imag = value[:ROWS], value[ROWS:]
-        value = jnp.concatenate(
-            [real * turn[0] - imag * turn[1], real * turn[1] + imag * turn[0]], axis=1
-        )
-        high, low = halves_of(value)
+                mixed_out[c, peer * 16 : peer * 16 + 16] = relay[pl.ds(peer, 16, stride=16), :].astype(BF16)
+            exchange(
+                rows_of(mixed_out.at[c]), rows_of(mixed_in.at[c]), mixed_send.at[c],
+                mixed_recv.at[c],
+            )
+
+    def transformed(signals):
+        wide = jnp.concatenate(signals, axis=1)
+        value = dot(first[0], wide) + dot(first[1], wide)
+        parts = []
+        for n in range(len(signals)):
+            real = value[:ROWS, n * COLS : (n + 1) * COLS]
+            imag = value[ROWS:, n * COLS : (n + 1) * COLS]
+            parts.append(
+                jnp.concatenate(
+                    [real * turn[0] - imag * turn[1], real * turn[1] + imag * turn[0]], axis=1
+                )
+            )
+        high, low = halves_of(jnp.concatenate(parts, axis=0))
         return dot(high, ahead[0]) + dot(high, ahead[1]) + dot(low, ahead[0])
 
-    def send_taps():
+    def arrange_taps():
         taps_load.wait()
         for q in range(MIXES):
             for h in range(2):
                 spread(taps[q * 16 : q * 16 + 16, h * HALF : (h + 1) * HALF].astype(F32), h)
             for peer in range(16):
                 taps_out[peer, q] = relay[pl.ds(peer, 16, stride=16), :].astype(BF16)
-        exchange(taps_out, taps_in, taps_send, taps_recv)
+
+    def send_taps():
+        exchange(lambda peer: taps_out.at[peer], lambda peer: taps_in.at[peer], taps_send, taps_recv)
 
     def filter_spectra():
         exchange_arrived(taps_out, taps_in, taps_recv)
         for copy in table_loads:
             copy.wait()
-        for q in range(MIXES):
-            spectrum[q] = transformed(taps_in[:, q].reshape(ROWS, COLS))
+        value = transformed([taps_in[:, q].reshape(ROWS, COLS) for q in range(MIXES)])
+        spectrum[...] = value.reshape(MIXES, ROWS, 2 * COLS)
 
     def convolve(q):
         exchange_arrived(mixed_out.at[q], mixed_in.at[q], mixed_recv.at[q])
-        value = transformed(mixed_in[q].reshape(ROWS, COLS))
+        value = transformed([mixed_in[q]])
         real, imag = value[:, :COLS], value[:, COLS:]
         freal, fimag = spectrum[q, :, :COLS], spectrum[q, :, COLS:]
         value = jnp.concatenate(
@@ -265,53 +279,64 @@
             [real * turn[0] + imag * turn[1], imag * turn[0] - real * turn[1]], axis=0
         )
         high, low = halves_of(value)
-        value = dot(last[0], high) + dot(last[0], low) + dot(last[1], high)
-        conv_out[q] = value.reshape(16, 16, COLS)
-        exchange(conv_out.at[q], conv_in.at[q], conv_send.at[q], conv_recv.at[q])
+        conv_out[q] = dot(last[0], high) + dot(last[0], low) + dot(last[1], high)
+        exchange(rows_of(conv_out.at[q]), rows_of(conv_in.at[q]), conv_send.at[q], conv_recv.at[q])
 
     def emit(q):
         exchange_arrived(conv_out.at[q], conv_in.at[q], conv_recv.at[q])
-        relay[...] = conv_in[q].reshape(256, COLS)
         rows = pl.ds(q * 16, 16)
         for tile in range(16):
             lanes = pl.ds(tile * COLS, COLS)
-            part = relay[pl.ds(tile, 16, stride=16), :]
+            part = conv_in[q, pl.ds(tile, 16, stride=16), :]
             gated[rows, lanes] = (gates[rows, lanes] * part).astype(BF16)
         pltpu.make_async_copy(gated.at[rows], out_hbm.at[rows], store_sem.at[q]).start()
 
     turn_weights(1)
     turn_weights(2)
-    pl.semaphore_wait(barrier, 3 + blocks - 1)
     multiply(0)
+    multiply(1)
+    pl.semaphore_wait(barrier, 7)
+    for near in around:
+        signal(near_sem, near)
+    core_go(0)
+    core_go(1)
+    multiply(2)
+    core_go(2)
+    arrange_taps()
+    combine(0)
+    combine(1)
+    pl.semaphore_wait(near_sem, 4)
+    for far in across:
+        signal(far_sem, far)
+    turn_weights(0)
+    pass_on(0)
+    multiply(3)
+    core_go(3)
+    pl.semaphore_wait(far_sem, 2)
     send_taps()
-    multiply(1)
-    combine(0)
-    turn_weights(0)
-    multiply(2)
-    pass_on(0)
-    combine(1)
+    combine(2)
+    pass_on(1)
+    finish(0)
+    multiply(4)
+    core_go(4)
     filter_spectra()
-    finish(0)
-    multiply(3)
-    pass_on(1)
-    combine(2)
+    combine(3)
+    pass_on(2)
     finish(1)
     convolve(0)
-    multiply(4)
-    pass_on(2)
-    combine(3)
-    finish(2)
-    convolve(1)
-    multiply(5)
     pass_on(3)
     combine(4)
+    finish(2)
+    multiply(5)
+    core_go(5)
+    convolve(1)
+    combine(5)
+    pass_on(4)
     finish(3)
     convolve(2)
-    pass_on(4)
-    combine(5)
+    pass_on(5)
+    convolve(3)
     finish(4)
-    convolve(3)
-    pass_on(5)
     emit(0)
     emit(1)
     finish(5)
@@ -323,10 +348,10 @@
             core_copy(c, h).wait_send()
         for kind in range(6):
             ring_copy(c, kind).wait_send()
-    exchange_left(taps_out, taps_in, taps_send)
+    exchange_left(taps_out, taps_in, taps_send, blocks - 1)
     for q in range(MIXES):
-        exchange_left(mixed_out.at[q], mixed_in.at[q], mixed_send.at[q])
-        exchange_left(conv_out.at[q], conv_in.at[q], conv_send.at[q])
+        exchange_left(mixed_out.at[q], mixed_in.at[q], mixed_send.at[q], (blocks - 1) * 16)
+        exchange_left(conv_out.at[q], conv_in.at[q], conv_send.at[q], (blocks - 1) * 16)
         rows = pl.ds(q * 16, 16)
         pltpu.make_async_copy(gated.at[rows], out_hbm.at[rows], store_sem.at[q]).wait()
 
@@ -357,11 +382,11 @@
             pltpu.VMEM((256, COLS), F32),
             pltpu.VMEM((blocks, MIXES, 16, COLS), BF16),
             pltpu.VMEM((blocks, MIXES, 16, COLS), BF16),
-            pltpu.VMEM((MIXES, blocks, 16, COLS), BF16),
-            pltpu.VMEM((MIXES, blocks, 16, COLS), BF16),
+            pltpu.VMEM((MIXES, ROWS, COLS), BF16),
+            pltpu.VMEM((MIXES, ROWS, COLS), BF16),
             pltpu.VMEM((MIXES, ROWS, 2 * COLS), F32),
-            pltpu.VMEM((MIXES, blocks, 16, COLS), F32),
-            pltpu.VMEM((MIXES, blocks, 16, COLS), F32),
+            pltpu.VMEM((MIXES, ROWS, COLS), F32),
+            pltpu.VMEM((MIXES, ROWS, COLS), F32),
             pltpu.VMEM(filter_taps.shape, F32),
             pltpu.VMEM(filter_taps.shape, BF16),
             dma((11,)),
@@ -376,6 +401,8 @@
             dma((MIXES,)),
             dma((MIXES,)),
             dma((MIXES,)),
+            pltpu.SemaphoreType.REGULAR,
+            pltpu.SemaphoreType.REGULAR,
         ],
         compiler_params=pltpu.CompilerParams(
             collective_id=0, has_side_effects=True, vmem_limit_bytes=60 * 1024 * 1024

time: 60.8 us -> 48.6 us (0.80)
  Pallas kernels: 59 us -> 46.8 us
    pallas_call x1, Pallas kernels: 59 us -> 46.8 us  [per_device(): pl.pallas_call(kernel, out_shape=jax.ShapeDtypeStruct(filter_taps.shape,...]
where the time goes in v3:
time: 48.6 us; the launch traced here: 48.5 us
  Pallas kernels  46.8 us (96%)
  local copies, waits for them, and re-layouts  1.67 us (3%)
    pallas_call x1, Pallas kernels, per_device(): pl.pallas_call(kernel, out_shape=jax.ShapeDtypeStruct(filter_taps.shape,...  46.8 us
    unnamed x1, local copies, waits for them, and re-layouts  1.67 us

profile of v3, /device:TPU:0, one launch (start us, length us, event | category | flops | bytes accessed | tf_op | source)
XLA Modules:
  0.0 48.5 jit_solution(8652963952539836093)
XLA Ops:
  0.0 46.8 %shard_map.82 = bf16[64,2048]{1,0:T(8,128)(2,1)} custom-call(bf16[2048,1024]{1,0:T(8,128)(2,1)} %hidden_hbm.1, bf16[3,1024,512]{2,1,0:T(8,128)(2,1)} %proj_hbm.1, bf16[64,2048]{1,0:T(8,128)(2,1)} %taps_hbm.1, bf16[2,512,256]{2,1,0:T(8,128)(2,1)} %constant.10.clone.first_hbm, bf16[2,256,256]{2,1,0:T(8,128)(2,1)} %constant.11.clone.ahead_hbm, ...), custom_call_target="tpu_custom_call" | custom-call | flops 7000000000 | bytes 8000000 | tf_op jit(solution)/shard_map/pallas_call | solution.py:364
  46.8 1.7 %copy.10 = bf16[64,2048]{1,0:T(8,128)(2,1)} copy(bf16[64,2048]{1,0:T(8,128)(2,1)} %shard_map.82) | data formatting | bytes 524288

commit v4 on v3

--- a/solution.py
+++ b/solution.py
@@ -61,7 +61,7 @@
     weights, own, core_out, core_in, ring_out, ring_in,
     relay, taps_out, taps_in, mixed_out, mixed_in, spectrum, conv_out, conv_in, gates, gated,
     load_sem, core_send, core_recv, ring_send, ring_recv,
-    taps_send, taps_recv, mixed_send, mixed_recv, conv_send, conv_recv, store_sem, near_sem, far_sem,
+    taps_send, taps_recv, mixed_send, mixed_recv, conv_send, conv_recv, store_sem, walk_sem,
 ):
     seq = lax.axis_index("seq")
     chan = lax.axis_index("chan")
@@ -72,6 +72,22 @@
     right = {"chan": lax.rem(y + 1, 4) * 2 + core}
     left = {"chan": lax.rem(y + 3, 4) * 2 + core}
 
+    def signal(semaphore, device):
+        pl.semaphore_signal(
+            semaphore, inc=1, device_id=device, device_id_type=pl.DeviceIdType.MESH
+        )
+
+    side = 4
+    z, x = seq // side, lax.rem(seq, side)
+    odd = lax.rem(z, 2)
+    place = z * side + x + odd * (side - 1 - 2 * x)
+
+    def walk(by):
+        spot = lax.rem(place + by + blocks, blocks)
+        row, col = spot // side, lax.rem(spot, side)
+        flipped = lax.rem(row, 2)
+        return {"seq": row * side + col + flipped * (side - 1 - 2 * col)}
+
     loads = []
 
     def load(src, dst):
@@ -85,6 +101,9 @@
         load(hidden_hbm.at[pl.ds(n * HALF, HALF)], hidden.at[pl.ds(n * HALF, HALF)])
         for n in range(2)
     ]
+    barrier = pltpu.get_barrier_semaphore()
+    for device in (right, left, walk(1), partner):
+        signal(barrier, device)
     taps_load = load(taps_hbm, taps)
     proj_loads[0] = load(proj_hbm.at[0], proj.at[0])
     table_loads = [
@@ -95,22 +114,14 @@
         load(turn_hbm, turn),
     ]
 
-    def signal(semaphore, device):
-        pl.semaphore_signal(
-            semaphore, inc=1, device_id=device, device_id_type=pl.DeviceIdType.MESH
-        )
-
-    side = 4
-    z, x = seq // side, lax.rem(seq, side)
-
-    def plane(by_z, by_x):
-        return {"seq": lax.rem(z + by_z, side) * side + lax.rem(x + by_x, side)}
-
-    around = [plane(0, 1), plane(0, side - 1), plane(1, 0), plane(side - 1, 0)]
-    across = [plane(0, 2), plane(2, 0)]
-    barrier = pltpu.get_barrier_semaphore()
-    for near in [partner, right, left] + around:
-        signal(barrier, near)
+    rounds = ((-1,), (-1, 1), (-2, 2), (-4, 4))
+
+    def tell(n):
+        for by in rounds[n]:
+            signal(walk_sem.at[n], walk(by))
+
+    def hear(n):
+        pl.semaphore_wait(walk_sem.at[n], len(rounds[n]))
 
     def remote(src, dst, send, recv, device):
         return pltpu.make_async_remote_copy(
@@ -121,10 +132,12 @@
     def exchange(src, dst, send, recv):
         pltpu.make_async_copy(src(seq), dst(seq), recv).start()
 
-        @pl.loop(1, blocks)
-        def _(step):
-            peer = lax.rem(seq + step, blocks)
+        def send_to(step):
+            peer = lax.rem(z + step // side, side) * side + lax.rem(x + step, side)
             remote(src(peer), dst(seq), send, recv, {"seq": peer}).start()
+
+        pl.loop(10, blocks)(send_to)
+        pl.loop(1, 10)(lambda step: send_to(10 - step))
 
     def exchange_arrived(src, dst, recv):
         pltpu.make_async_copy(src, dst, recv).wait()
@@ -161,10 +174,18 @@
                             side * 64 + 16 * part : side * 64 + 16 * part + 16
                         ]
 
-    def core_copy(c, h):
+    pieces = ((2, 0), (2, 1), (1, 1), (3, 0), (1, 0), (3, 1), (0, 0), (0, 1))
+    groups = ((0, 2), (2, 2), (4, 4))
+
+    def core_copy(c, group):
+        part = pl.ds(*groups[group])
         return remote(
-            core_out.at[c, h], core_in.at[c, h], core_send.at[c, h], core_recv.at[c, h], partner
-        )
+            core_out.at[c, part], core_in.at[c, part], core_send.at[c, group],
+            core_recv.at[c, group], partner,
+        )
+
+    def summed(c, piece):
+        return own[c, piece] + core_in[c, piece].astype(F32)
 
     def ring_copy(c, kind):
         return remote(
@@ -180,43 +201,38 @@
                 weights[c], hidden[h * HALF : (h + 1) * HALF],
                 (((1,), (1,)), ((), ())), preferred_element_type=F32,
             )
-            core_out[c, h] = product[:128].astype(BF16)
-            own[c, h] = product[128:]
+            for piece, (owner, half) in enumerate(pieces):
+                if half == h:
+                    core_out[c, piece] = product[owner * 32 : owner * 32 + 32].astype(BF16)
+                    own[c, piece] = product[128 + owner * 32 : 160 + owner * 32]
 
     def core_go(c):
-        for h in range(2):
-            core_copy(c, h).start()
-
-    def combine(c):
-        def summed(h, row):
-            return own[c, h, row : row + 32] + core_in[c, h, row : row + 32].astype(F32)
-
-        for h in range(2):
-            core_copy(c, h).wait_recv()
-            ring_out[c, h] = summed(h, 64).astype(BF16)
-            ring_copy(c, h).start()
-        for h in range(2):
-            kind = 3 if h == 0 else 2
-            ring_out[c, kind] = summed(h, 96 if h == 0 else 32).astype(BF16)
+        for group in range(3):
+            core_copy(c, group).start()
+
+    def send_pieces(c, group):
+        core_copy(c, group).wait_recv()
+        for kind in (2 * group, 2 * group + 1):
+            ring_out[c, kind] = summed(c, kind).astype(BF16)
             ring_copy(c, kind).start()
-        for h in range(2):
-            for row in (32 if h == 0 else 96, 0):
-                own[c, h, row : row + 32] = summed(h, row)
+
+    def far(c):
+        send_pieces(c, 0)
+
+    def near(c):
+        send_pieces(c, 1)
 
     def pass_on(c):
+        core_copy(c, 2).wait_recv()
         for h in range(2):
             ring_copy(c, h).wait_recv()
-            later = 32 if h == 0 else 96
-            ring_out[c, 4 + h] = (
-                own[c, h, later : later + 32] + ring_in[c, h].astype(F32)
-            ).astype(BF16)
+            ring_out[c, 4 + h] = (summed(c, 4 + h) + ring_in[c, h].astype(F32)).astype(BF16)
             ring_copy(c, 4 + h).start()
 
     def finish(c):
         for h in range(2):
-            kinds = (3, 4) if h == 0 else (2, 5)
-            total = own[c, h, 0:32]
-            for kind in kinds:
+            total = summed(c, 6 + h)
+            for kind in (3, 4) if h == 0 else (2, 5):
                 ring_copy(c, kind).wait_recv()
                 total = total + ring_in[c, kind].astype(F32)
             if c >= MIXES:
@@ -225,7 +241,9 @@
                 spread(total[:16] * total[16:], h)
         if c < MIXES:
             for peer in range(16):
-                mixed_out[c, peer * 16 : peer * 16 + 16] = relay[pl.ds(peer, 16, stride=16), :].astype(BF16)
+                mixed_out[c, peer * 16 : peer * 16 + 16] = relay[
+                    pl.ds(peer, 16, stride=16), :
+                ].astype(BF16)
             exchange(
                 rows_of(mixed_out.at[c]), rows_of(mixed_in.at[c]), mixed_send.at[c],
                 mixed_recv.at[c],
@@ -294,45 +312,53 @@
     turn_weights(1)
     turn_weights(2)
     multiply(0)
+    pl.semaphore_wait(barrier, 4)
+    core_go(0)
+    tell(0)
     multiply(1)
-    pl.semaphore_wait(barrier, 7)
-    for near in around:
-        signal(near_sem, near)
-    core_go(0)
     core_go(1)
+    far(0)
+    near(0)
+    hear(0)
+    tell(1)
     multiply(2)
     core_go(2)
+    far(1)
+    hear(1)
+    tell(2)
     arrange_taps()
-    combine(0)
-    combine(1)
-    pl.semaphore_wait(near_sem, 4)
-    for far in across:
-        signal(far_sem, far)
     turn_weights(0)
-    pass_on(0)
     multiply(3)
     core_go(3)
-    pl.semaphore_wait(far_sem, 2)
-    send_taps()
-    combine(2)
-    pass_on(1)
-    finish(0)
+    pass_on(0)
+    near(1)
+    far(2)
+    hear(2)
+    tell(3)
     multiply(4)
     core_go(4)
-    filter_spectra()
-    combine(3)
-    pass_on(2)
-    finish(1)
-    convolve(0)
-    pass_on(3)
-    combine(4)
-    finish(2)
+    hear(3)
+    send_taps()
+    pass_on(1)
+    near(2)
+    far(3)
     multiply(5)
     core_go(5)
+    finish(0)
+    pass_on(2)
+    near(3)
+    filter_spectra()
+    finish(1)
+    pass_on(3)
+    far(4)
+    near(4)
+    convolve(0)
+    finish(2)
+    far(5)
+    finish(3)
     convolve(1)
-    combine(5)
     pass_on(4)
-    finish(3)
+    near(5)
     convolve(2)
     pass_on(5)
     convolve(3)
@@ -344,8 +370,8 @@
     emit(3)
 
     for c in range(CHUNKS):
-        for h in range(2):
-            core_copy(c, h).wait_send()
+        for group in range(3):
+            core_copy(c, group).wait_send()
         for kind in range(6):
             ring_copy(c, kind).wait_send()
     exchange_left(taps_out, taps_in, taps_send, blocks - 1)
@@ -374,9 +400,9 @@
         + [pltpu.VMEM(table.shape, table.dtype) for table in tables]
         + [
             pltpu.VMEM((CHUNKS, 256, hidden_in.shape[1]), BF16),
-            pltpu.VMEM((CHUNKS, 2, 128, HALF), F32),
-            pltpu.VMEM((CHUNKS, 2, 128, HALF), BF16),
-            pltpu.VMEM((CHUNKS, 2, 128, HALF), BF16),
+            pltpu.VMEM((CHUNKS, 8, 32, HALF), F32),
+            pltpu.VMEM((CHUNKS, 8, 32, HALF), BF16),
+            pltpu.VMEM((CHUNKS, 8, 32, HALF), BF16),
             pltpu.VMEM((CHUNKS, 6, 32, HALF), BF16),
             pltpu.VMEM((CHUNKS, 6, 32, HALF), BF16),
             pltpu.VMEM((256, COLS), F32),
@@ -390,8 +416,8 @@
             pltpu.VMEM(filter_taps.shape, F32),
             pltpu.VMEM(filter_taps.shape, BF16),
             dma((11,)),
-            dma((CHUNKS, 2)),
-            dma((CHUNKS, 2)),
+            dma((CHUNKS, 3)),
+            dma((CHUNKS, 3)),
             dma((CHUNKS, 6)),
             dma((CHUNKS, 6)),
             dma(()),
@@ -401,8 +427,7 @@
             dma((MIXES,)),
             dma((MIXES,)),
             dma((MIXES,)),
-            pltpu.SemaphoreType.REGULAR,
-            pltpu.SemaphoreType.REGULAR,
+            pltpu.SemaphoreType.REGULAR((4,)),
         ],
         compiler_params=pltpu.CompilerParams(
             collective_id=0, has_side_effects=True, vmem_limit_bytes=60 * 1024 * 1024

time: 48.6 us -> 44.4 us (0.914)
  Pallas kernels: 46.8 us -> 42.6 us
    pallas_call x1, Pallas kernels: 46.8 us -> 42.6 us  [per_device(): pl.pallas_call(kernel, out_shape=jax.ShapeDtypeStruct(filter_taps.shape,...]
where the time goes in v4:
time: 44.4 us; the launch traced here: 44.2 us
  Pallas kernels  42.6 us (96%)
  local copies, waits for them, and re-layouts  1.67 us (4%)
    pallas_call x1, Pallas kernels, per_device(): pl.pallas_call(kernel, out_shape=jax.ShapeDtypeStruct(filter_taps.shape,...  42.6 us
    unnamed x1, local copies, waits for them, and re-layouts  1.67 us

profile of v4, /device:TPU:0, one launch (start us, length us, event | category | flops | bytes accessed | tf_op | source)
XLA Modules:
  0.0 44.2 jit_solution(3624579141509234531)
XLA Ops:
  0.0 42.6 %shard_map.82 = bf16[64,2048]{1,0:T(8,128)(2,1)} custom-call(bf16[2048,1024]{1,0:T(8,128)(2,1)} %hidden_hbm.1, bf16[3,1024,512]{2,1,0:T(8,128)(2,1)} %proj_hbm.1, bf16[64,2048]{1,0:T(8,128)(2,1)} %taps_hbm.1, bf16[2,512,256]{2,1,0:T(8,128)(2,1)} %constant.10.clone.first_hbm, bf16[2,256,256]{2,1,0:T(8,128)(2,1)} %constant.11.clone.ahead_hbm, ...), custom_call_target="tpu_custom_call" | custom-call | flops 7000000000 | bytes 8000000 | tf_op jit(solution)/shard_map/pallas_call | solution.py:390
  42.6 1.7 %copy.10 = bf16[64,2048]{1,0:T(8,128)(2,1)} copy(bf16[64,2048]{1,0:T(8,128)(2,1)} %shard_map.82) | data formatting | bytes 524288

commit v5 on v4

--- a/solution.py
+++ b/solution.py
@@ -90,9 +90,10 @@
 
     loads = []
 
-    def load(src, dst):
+    def load(src, dst, now=True):
         copy = pltpu.make_async_copy(src, dst, load_sem.at[len(loads)])
-        copy.start()
+        if now:
+            copy.start()
         loads.append(copy)
         return copy
 
@@ -104,15 +105,19 @@
     barrier = pltpu.get_barrier_semaphore()
     for device in (right, left, walk(1), partner):
         signal(barrier, device)
-    taps_load = load(taps_hbm, taps)
-    proj_loads[0] = load(proj_hbm.at[0], proj.at[0])
+    taps_load = load(taps_hbm, taps, False)
+    proj_loads[0] = load(proj_hbm.at[0], proj.at[0], False)
     table_loads = [
-        load(first_hbm, first),
-        load(ahead_hbm, ahead),
-        load(back_hbm, back),
-        load(last_hbm, last),
-        load(turn_hbm, turn),
+        load(first_hbm, first, False),
+        load(ahead_hbm, ahead, False),
+        load(back_hbm, back, False),
+        load(last_hbm, last, False),
+        load(turn_hbm, turn, False),
     ]
+
+    def load_rest():
+        for copy in loads[4:]:
+            copy.start()
 
     rounds = ((-1,), (-1, 1), (-2, 2), (-4, 4))
 
@@ -129,15 +134,19 @@
             device_id=device, device_id_type=pl.DeviceIdType.MESH,
         )
 
+    def hops(step):
+        return sum(min(by, side - by) for by in divmod(step, side))
+
+    peers = [
+        lax.rem(z + step // side, side) * side + lax.rem(x + step % side, side)
+        for step in sorted(range(1, side * side), key=hops, reverse=True)
+    ]
+
     def exchange(src, dst, send, recv):
         pltpu.make_async_copy(src(seq), dst(seq), recv).start()
 
-        def send_to(step):
-            peer = lax.rem(z + step // side, side) * side + lax.rem(x + step, side)
+        for peer in peers:
             remote(src(peer), dst(seq), send, recv, {"seq": peer}).start()
-
-        pl.loop(10, blocks)(send_to)
-        pl.loop(1, 10)(lambda step: send_to(10 - step))
 
     def exchange_arrived(src, dst, recv):
         pltpu.make_async_copy(src, dst, recv).wait()
@@ -175,10 +184,11 @@
                         ]
 
     pieces = ((2, 0), (2, 1), (1, 1), (3, 0), (1, 0), (3, 1), (0, 0), (0, 1))
-    groups = ((0, 2), (2, 2), (4, 4))
+    def groups(c):
+        return ((0, 2), (2, 2), (4, 4)) if c == 0 else ((0, 8),)
 
     def core_copy(c, group):
-        part = pl.ds(*groups[group])
+        part = pl.ds(*groups(c)[group])
         return remote(
             core_out.at[c, part], core_in.at[c, part], core_send.at[c, group],
             core_recv.at[c, group], partner,
@@ -207,11 +217,12 @@
                     own[c, piece] = product[128 + owner * 32 : 160 + owner * 32]
 
     def core_go(c):
-        for group in range(3):
+        for group in range(len(groups(c))):
             core_copy(c, group).start()
 
     def send_pieces(c, group):
-        core_copy(c, group).wait_recv()
+        if group < len(groups(c)):
+            core_copy(c, group).wait_recv()
         for kind in (2 * group, 2 * group + 1):
             ring_out[c, kind] = summed(c, kind).astype(BF16)
             ring_copy(c, kind).start()
@@ -223,7 +234,8 @@
         send_pieces(c, 1)
 
     def pass_on(c):
-        core_copy(c, 2).wait_recv()
+        if c == 0:
+            core_copy(c, 2).wait_recv()
         for h in range(2):
             ring_copy(c, h).wait_recv()
             ring_out[c, 4 + h] = (summed(c, 4 + h) + ring_in[c, h].astype(F32)).astype(BF16)
@@ -297,15 +309,17 @@
             [real * turn[0] + imag * turn[1], imag * turn[0] - real * turn[1]], axis=0
         )
         high, low = halves_of(value)
-        conv_out[q] = dot(last[0], high) + dot(last[0], low) + dot(last[1], high)
+        value = dot(last[0], high) + dot(last[0], low) + dot(last[1], high)
+        conv_out[q] = value.astype(BF16)
         exchange(rows_of(conv_out.at[q]), rows_of(conv_in.at[q]), conv_send.at[q], conv_recv.at[q])
 
     def emit(q):
         exchange_arrived(conv_out.at[q], conv_in.at[q], conv_recv.at[q])
         rows = pl.ds(q * 16, 16)
+        relay[...] = conv_in[q].astype(F32)
         for tile in range(16):
             lanes = pl.ds(tile * COLS, COLS)
-            part = conv_in[q, pl.ds(tile, 16, stride=16), :]
+            part = relay[pl.ds(tile, 16, stride=16), :]
             gated[rows, lanes] = (gates[rows, lanes] * part).astype(BF16)
         pltpu.make_async_copy(gated.at[rows], out_hbm.at[rows], store_sem.at[q]).start()
 
@@ -314,6 +328,7 @@
     multiply(0)
     pl.semaphore_wait(barrier, 4)
     core_go(0)
+    load_rest()
     tell(0)
     multiply(1)
     core_go(1)
@@ -352,13 +367,13 @@
     pass_on(3)
     far(4)
     near(4)
+    far(5)
+    near(5)
     convolve(0)
     finish(2)
-    far(5)
     finish(3)
     convolve(1)
     pass_on(4)
-    near(5)
     convolve(2)
     pass_on(5)
     convolve(3)
@@ -370,7 +385,7 @@
     emit(3)
 
     for c in range(CHUNKS):
-        for group in range(3):
+        for group in range(len(groups(c))):
             core_copy(c, group).wait_send()
         for kind in range(6):
             ring_copy(c, kind).wait_send()
@@ -411,8 +426,8 @@
             pltpu.VMEM((MIXES, ROWS, COLS), BF16),
             pltpu.VMEM((MIXES, ROWS, COLS), BF16),
             pltpu.VMEM((MIXES, ROWS, 2 * COLS), F32),
-            pltpu.VMEM((MIXES, ROWS, COLS), F32),
-            pltpu.VMEM((MIXES, ROWS, COLS), F32),
+            pltpu.VMEM((MIXES, ROWS, COLS), BF16),
+            pltpu.VMEM((MIXES, ROWS, COLS), BF16),
             pltpu.VMEM(filter_taps.shape, F32),
             pltpu.VMEM(filter_taps.shape, BF16),
             dma((11,)),

time: 44.4 us -> 44 us (level)
  no operation moved by 1% of the time
where the time goes in v5:
time: 44 us; the launch traced here: 43.9 us
  Pallas kernels  42.2 us (96%)
  local copies, waits for them, and re-layouts  1.67 us (4%)
    pallas_call x1, Pallas kernels, per_device(): pl.pallas_call(kernel, out_shape=jax.ShapeDtypeStruct(filter_taps.shape,...  42.2 us
    unnamed x1, local copies, waits for them, and re-layouts  1.67 us

profile of v5, /device:TPU:0, one launch (start us, length us, event | category | flops | bytes accessed | tf_op | source)
XLA Modules:
  0.0 43.9 jit_solution(2907404710693080331)
XLA Ops:
  0.0 42.2 %shard_map.82 = bf16[64,2048]{1,0:T(8,128)(2,1)} custom-call(bf16[2048,1024]{1,0:T(8,128)(2,1)} %hidden_hbm.1, bf16[3,1024,512]{2,1,0:T(8,128)(2,1)} %proj_hbm.1, bf16[64,2048]{1,0:T(8,128)(2,1)} %taps_hbm.1, bf16[2,512,256]{2,1,0:T(8,128)(2,1)} %constant.10.clone.first_hbm, bf16[2,256,256]{2,1,0:T(8,128)(2,1)} %constant.11.clone.ahead_hbm, ...), custom_call_target="tpu_custom_call" | custom-call | flops 7000000000 | bytes 8000000 | tf_op jit(solution)/shard_map/pallas_call | solution.py:405
  42.2 1.7 %copy.10 = bf16[64,2048]{1,0:T(8,128)(2,1)} copy(bf16[64,2048]{1,0:T(8,128)(2,1)} %shard_map.82) | data formatting | bytes 524288

commit v6 on v5

--- a/solution.py
+++ b/solution.py
@@ -61,7 +61,7 @@
     weights, own, core_out, core_in, ring_out, ring_in,
     relay, taps_out, taps_in, mixed_out, mixed_in, spectrum, conv_out, conv_in, gates, gated,
     load_sem, core_send, core_recv, ring_send, ring_recv,
-    taps_send, taps_recv, mixed_send, mixed_recv, conv_send, conv_recv, store_sem, walk_sem,
+    taps_send, taps_recv, mixed_send, mixed_recv, conv_send, conv_recv, store_sem,
 ):
     seq = lax.axis_index("seq")
     chan = lax.axis_index("chan")
@@ -79,14 +79,6 @@
 
     side = 4
     z, x = seq // side, lax.rem(seq, side)
-    odd = lax.rem(z, 2)
-    place = z * side + x + odd * (side - 1 - 2 * x)
-
-    def walk(by):
-        spot = lax.rem(place + by + blocks, blocks)
-        row, col = spot // side, lax.rem(spot, side)
-        flipped = lax.rem(row, 2)
-        return {"seq": row * side + col + flipped * (side - 1 - 2 * col)}
 
     loads = []
 
@@ -103,8 +95,10 @@
         for n in range(2)
     ]
     barrier = pltpu.get_barrier_semaphore()
-    for device in (right, left, walk(1), partner):
+    for device in (right, left, partner):
         signal(barrier, device)
+    for by in range(1, side * side):
+        signal(barrier, {"seq": lax.rem(seq + by, blocks)})
     taps_load = load(taps_hbm, taps, False)
     proj_loads[0] = load(proj_hbm.at[0], proj.at[0], False)
     table_loads = [
@@ -118,15 +112,6 @@
     def load_rest():
         for copy in loads[4:]:
             copy.start()
-
-    rounds = ((-1,), (-1, 1), (-2, 2), (-4, 4))
-
-    def tell(n):
-        for by in rounds[n]:
-            signal(walk_sem.at[n], walk(by))
-
-    def hear(n):
-        pl.semaphore_wait(walk_sem.at[n], len(rounds[n]))
 
     def remote(src, dst, send, recv, device):
         return pltpu.make_async_remote_copy(
@@ -326,43 +311,35 @@
     turn_weights(1)
     turn_weights(2)
     multiply(0)
-    pl.semaphore_wait(barrier, 4)
+    pl.semaphore_wait(barrier, 18)
     core_go(0)
     load_rest()
-    tell(0)
     multiply(1)
     core_go(1)
     far(0)
     near(0)
-    hear(0)
-    tell(1)
     multiply(2)
     core_go(2)
+    arrange_taps()
+    send_taps()
     far(1)
-    hear(1)
-    tell(2)
-    arrange_taps()
     turn_weights(0)
     multiply(3)
     core_go(3)
     pass_on(0)
     near(1)
     far(2)
-    hear(2)
-    tell(3)
     multiply(4)
     core_go(4)
-    hear(3)
-    send_taps()
     pass_on(1)
     near(2)
     far(3)
     multiply(5)
     core_go(5)
+    filter_spectra()
     finish(0)
     pass_on(2)
     near(3)
-    filter_spectra()
     finish(1)
     pass_on(3)
     far(4)
@@ -442,7 +419,6 @@
             dma((MIXES,)),
             dma((MIXES,)),
             dma((MIXES,)),
-            pltpu.SemaphoreType.REGULAR((4,)),
         ],
         compiler_params=pltpu.CompilerParams(
             collective_id=0, has_side_effects=True, vmem_limit_bytes=60 * 1024 * 1024

time: 44 us -> 43.9 us (level)
  no operation moved by 1% of the time
where the time goes in v6:
time: 43.9 us; the launch traced here: 43.8 us
  Pallas kernels  42.1 us (96%)
  local copies, waits for them, and re-layouts  1.67 us (4%)
    pallas_call x1, Pallas kernels, per_device(): pl.pallas_call(kernel, out_shape=jax.ShapeDtypeStruct(filter_taps.shape,...  42.1 us
    unnamed x1, local copies, waits for them, and re-layouts  1.67 us

profile of v6, /device:TPU:0, one launch (start us, length us, event | category | flops | bytes accessed | tf_op | source)
XLA Modules:
  0.0 43.8 jit_solution(1368919129579143295)
XLA Ops:
  0.0 42.1 %shard_map.82 = bf16[64,2048]{1,0:T(8,128)(2,1)} custom-call(bf16[2048,1024]{1,0:T(8,128)(2,1)} %hidden_hbm.1, bf16[3,1024,512]{2,1,0:T(8,128)(2,1)} %proj_hbm.1, bf16[64,2048]{1,0:T(8,128)(2,1)} %taps_hbm.1, bf16[2,512,256]{2,1,0:T(8,128)(2,1)} %constant.10.clone.first_hbm, bf16[2,256,256]{2,1,0:T(8,128)(2,1)} %constant.11.clone.ahead_hbm, ...), custom_call_target="tpu_custom_call" | custom-call | flops 7000000000 | bytes 8000000 | tf_op jit(solution)/shard_map/pallas_call | solution.py:382
  42.1 1.7 %copy.10 = bf16[64,2048]{1,0:T(8,128)(2,1)} copy(bf16[64,2048]{1,0:T(8,128)(2,1)} %shard_map.82) | data formatting | bytes 524288
